TPU v7x, 32 devices: a whole 2x2x4 slice. The times are simulated.
32 devices in a mesh: packs: 4 (over x, core), seq: 8 (over z, y).
Axes of the slice: x: 2, y: 2, z: 4, core: 2. Of those that a mesh axis runs over, the one named last changes fastest.
Arguments:
- queries: bfloat16 [4096, 8192], P(('packs', 'seq')), parts along dimension 0, may hold values from -12 to 12
- keys: bfloat16 [4096, 1024], P(('packs', 'seq')), parts along dimension 0, may hold values from -6 to 6
- values: bfloat16 [4096, 1024], P(('packs', 'seq')), parts along dimension 0, may hold values from -6 to 6
- outputs: bfloat16 [4096, 8192], P(('packs', 'seq')), parts along dimension 0, may hold values from -6 to 6
- grad_out: bfloat16 [4096, 8192], P(('packs', 'seq')), parts along dimension 0, may hold values from -4 to 4
- lse_saved: float32 [4096, 64], P(('packs', 'seq')), parts along dimension 0, may hold values from -40 to 40
- doc_lengths: int32 [32], P('packs'), parts along dimension 0, may hold values from 1 to 512, as said below
Outputs:
- grad_queries: bfloat16 [4096, 8192], P(('packs', 'seq')), parts along dimension 0
- grad_keys: bfloat16 [4096, 1024], P(('packs', 'seq')), parts along dimension 0
- grad_values: bfloat16 [4096, 1024], P(('packs', 'seq')), parts along dimension 0
There are 4 independent parts, one for each index of `packs`. A program takes and returns all parts, laid end to end along the dimension named above; each array names one. Nothing has to cross between parts.
Inputs may be any that keep to these rules, and one draw needn't show every extreme that they name: `doc_lengths`: positive lengths summing to 1024; one document has exactly 512 tokens.
All inputs are finite; a program needn't handle non-finite values.
Results may differ from a plain program's by a relative error of at most 0.0049.
Values may be sent and summed in bfloat16 or wider, within the bound.
No kernel may reach another device: no remote copies, remote signals or barrier semaphores. Data moves between devices by JAX's collectives and lax.ppermute only.
A program may use at most 64 MiB of HBM per device.

v0:
```python
import functools

import jax
import jax.numpy as jnp
from jax import lax
from jax.experimental import pallas as pl
from jax.experimental.pallas import tpu as pltpu
from jax.sharding import PartitionSpec as P

HEADS = 64
KVH = 8
HDIM = 128
GROUP = HEADS // KVH
CHUNKS = (4, 4)
VMEM = 16 * 1024 * 1024


def contract_last(first, second):
    return lax.dot_general(
        first, second, (((1,), (1,)), ((), ())), preferred_element_type=jnp.float32
    )


def contract_first(first, second):
    return lax.dot_general(
        first, second, (((0,), (0,)), ((), ())), preferred_element_type=jnp.float32
    )


def head_rows(block):
    return jnp.concatenate(
        [block[:, h * HDIM : (h + 1) * HDIM] for h in range(GROUP)], axis=0
    )


def delta_kernel(out_ref, gout_ref, q_ref, delta_ref):
    rows = out_ref.shape[0]
    wide = GROUP * HDIM
    first = lax.broadcasted_iota(jnp.int32, (wide, HDIM), 1) * HDIM
    row = lax.broadcasted_iota(jnp.int32, (wide, HDIM), 0)
    ones = jnp.where((row >= first) & (row < first + HDIM), 1.0, 0.0).astype(jnp.bfloat16)
    for group in range(out_ref.shape[1] // wide):
        at = slice(group * wide, (group + 1) * wide)
        product = out_ref[:, at].astype(jnp.float32) * gout_ref[:, at].astype(jnp.float32)
        high = product.astype(jnp.bfloat16)
        low = (product - high.astype(jnp.float32)).astype(jnp.bfloat16)
        total = jnp.dot(high, ones, preferred_element_type=jnp.float32)
        total += jnp.dot(low, ones, preferred_element_type=jnp.float32)
        delta_ref[group * GROUP : (group + 1) * GROUP, :] = total.T[:GROUP]


def delta_rows(outputs, grad_out, queries):
    rows = outputs.shape[0]
    local = pl.BlockSpec(memory_space=pltpu.VMEM)
    return pl.pallas_call(
        delta_kernel,
        in_specs=[local] * 3,
        out_specs=local,
        out_shape=jax.ShapeDtypeStruct((HEADS, rows), jnp.float32),
        compiler_params=pltpu.CompilerParams(vmem_limit_bytes=VMEM),
        cost_estimate=pl.CostEstimate(
            flops=4 * rows * HEADS * HDIM * HDIM,
            bytes_accessed=6 * rows * HEADS * HDIM,
            transcendentals=0,
        ),
        name="delta",
    )(outputs, grad_out, queries)


def slot_shards(me, hops):
    side = lax.rem(me, 2)
    found = [me - 2 * hop for hop in range(hops + 1)]
    found += [me - 2 * hop + 1 - 2 * side for hop in range(1, hops)]
    found.append(jnp.where(side == 1, me - 1, me - 2 * hops + 1))
    return found


def attend_kernel(hops, joined, first, places, docs, q_ref, gout_ref, lse_ref, delta_ref, *refs):
    slots = 2 * hops + 1
    moved, refs = refs[:slots], refs[slots:]
    gq_ref, refs = refs[0], refs[1:]
    if joined:
        parts = refs[: hops + 1] + tuple(refs[hops + 1].at[hop] for hop in range(hops))
    else:
        parts = refs[:slots]
    k_all, v_all, bias, prob, score = refs[-5:]
    rows = q_ref.shape[0]
    scale = 1.0 / HDIM**0.5
    me = lax.axis_index("seq")

    token = lax.broadcasted_iota(jnp.int32, (1, rows), 1) + me * rows
    begin = jnp.zeros((1, rows), jnp.int32)
    bound = jnp.int32(0)
    for doc in range(docs.shape[0]):
        bound = bound + docs[doc]
        begin = jnp.where(token >= bound, bound, begin)
    row = lax.broadcasted_iota(jnp.int32, (rows, rows), 0)
    for slot, shard in enumerate(slot_shards(me, hops)):
        key = row + shard * rows
        visible = (key <= token) & (key >= begin)
        bias[slot * rows : (slot + 1) * rows, :] = jnp.where(visible, 0.0, -1e30)

    @pl.loop(0, moved[0].shape[-1] // HDIM)
    def _(index):
        column = pl.ds(pl.multiple_of(index * HDIM, HDIM), HDIM)
        wide = pl.ds(pl.multiple_of((first + index) * GROUP * HDIM, GROUP * HDIM), GROUP * HDIM)
        stat = pl.ds(pl.multiple_of((first + index) * GROUP, GROUP), GROUP)
        for slot in range(slots):
            here = slice(slot * rows, (slot + 1) * rows)
            pair = moved[slot] if places[slot] is None else moved[slot].at[places[slot]]
            k_all[here, :] = pair[0, :, column]
            v_all[here, :] = pair[1, :, column]
        queries = head_rows(q_ref[:, wide])
        gout = head_rows(gout_ref[:, wide])
        lses = lse_ref[stat, :]
        deltas = delta_ref[stat, :]
        keys = k_all[...]
        values = v_all[...]
        hidden = bias[...]
        hidden = jnp.concatenate([hidden, hidden], axis=1)
        for two in range(GROUP // 2):
            at = slice(2 * two * rows, (2 * two + 2) * rows)
            lse = jnp.concatenate([lses[2 * two : 2 * two + 1], lses[2 * two + 1 : 2 * two + 2]], axis=1)
            delta = jnp.concatenate(
                [deltas[2 * two : 2 * two + 1], deltas[2 * two + 1 : 2 * two + 2]], axis=1
            )
            raw = contract_last(keys, queries[at])
            attn = jnp.exp(raw * scale - lse + hidden)
            grad = contract_last(values, gout[at])
            prob[:, at] = attn.astype(jnp.bfloat16)
            score[:, at] = (attn * (grad - delta)).astype(jnp.bfloat16)
        scores = score[...]
        grad_k = jnp.dot(scores, queries, preferred_element_type=jnp.float32) * scale
        grad_v = jnp.dot(prob[...], gout, preferred_element_type=jnp.float32)
        for slot in range(slots):
            here = slice(slot * rows, (slot + 1) * rows)
            part = parts[slot]
            part[0, :, column] = grad_k[here].astype(part.dtype)
            part[1, :, column] = grad_v[here].astype(part.dtype)
        grad_q = (contract_first(keys, scores) * scale).astype(jnp.bfloat16)
        mine = pl.ds(pl.multiple_of(index * GROUP * HDIM, GROUP * HDIM), GROUP * HDIM)
        gq_ref[:, mine] = jnp.concatenate(
            [grad_q[:, h * rows : (h + 1) * rows].T for h in range(GROUP)], axis=1
        )


def attend(docs, queries, grad_out, lse, delta, moved, head, per, hops, joined):
    rows = queries.shape[0]
    slots = 2 * hops + 1
    local = pl.BlockSpec(memory_space=pltpu.VMEM)
    operands = [docs, queries, grad_out, lse, delta] + [array for array, index in moved]
    out_shape = [jax.ShapeDtypeStruct((rows, per * GROUP * HDIM), jnp.bfloat16)]
    kinds = [jnp.float32] + [jnp.bfloat16] * hops
    out_shape += [jax.ShapeDtypeStruct((2, rows, per * HDIM), kind) for kind in kinds]
    if joined:
        out_shape += [jax.ShapeDtypeStruct((hops, 2, rows, per * HDIM), jnp.bfloat16)]
    else:
        out_shape += [jax.ShapeDtypeStruct((2, rows, per * HDIM), jnp.bfloat16)] * hops
    pairs = slots * rows * rows * GROUP * per
    places = [index for array, index in moved]
    return pl.pallas_call(
        functools.partial(attend_kernel, hops, joined, head, places),
        in_specs=[pl.BlockSpec(memory_space=pltpu.SMEM)] + [local] * (len(operands) - 1),
        out_specs=[local] * len(out_shape),
        scratch_shapes=[
            pltpu.VMEM((slots * rows, HDIM), jnp.bfloat16),
            pltpu.VMEM((slots * rows, HDIM), jnp.bfloat16),
            pltpu.VMEM((slots * rows, rows), jnp.float32),
            pltpu.VMEM((slots * rows, GROUP * rows), jnp.bfloat16),
            pltpu.VMEM((slots * rows, GROUP * rows), jnp.bfloat16),
        ],
        out_shape=out_shape,
        compiler_params=pltpu.CompilerParams(vmem_limit_bytes=VMEM),
        cost_estimate=pl.CostEstimate(
            flops=40 * pairs * HDIM,
            bytes_accessed=per * rows * HDIM * 2 * (3 * GROUP + 6 * slots),
            transcendentals=pairs,
        ),
        name="attend",
    )(*operands)


def shards(queries, keys, values, outputs, grad_out, lse_saved, doc_lengths):
    seq = lax.axis_size("seq")
    me = lax.axis_index("seq").astype(jnp.int32)
    side = lax.rem(me, 2)
    hops = seq // 4
    def onward(hop):
        return [(s, s + 2) for s in range(2 * hop - 2, seq - 2)]

    def back(hop):
        return [(s, s - 2) for s in range(2 * hop, seq)]

    def to_odd(hop):
        return [(s, s + 1) for s in range(2 * hop, seq, 2)]

    def to_even(hop):
        return [(s + 1, s) for s in range(2 * hop, seq, 2)]

    def send(array, pairs):
        return lax.ppermute(array, "seq", pairs)

    def after(array, *others):
        return lax.optimization_barrier((array,) + others)[0]

    delta = delta_rows(outputs, grad_out, queries)
    lse = lse_saved.T
    heads = [sum(CHUNKS[:chunk]) for chunk in range(len(CHUNKS))]
    columns = []
    for head, per in zip(heads, CHUNKS):
        at = slice(head * HDIM, (head + per) * HDIM)
        own = jnp.stack([keys[:, at], values[:, at]])
        columns.append([own, send(own, onward(1))])
        columns[-1][1], delta = lax.optimization_barrier((columns[-1][1], delta))
    for column in columns:
        for hop in range(2, hops + 1):
            column.append(send(column[-1], onward(hop)))
    arrived = []
    for chunk, column in enumerate(columns):
        edge = jnp.where(side == 0, column[0], column[hops])
        moved = [(array, None) for array in column]
        if chunk == 0:
            crossed = [send(array, to_odd(1) + to_even(1)) for array in column[1:hops]]
            crossed.append(send(after(edge, *crossed), to_odd(0) + to_even(hops)))
            moved += [(array, None) for array in crossed]
        else:
            joint = jnp.stack(column[1:hops] + [edge])
            crossed = send(joint, to_odd(0) + to_even(1))
            moved += [(crossed, hop) for hop in range(hops)]
            arrived[0][-1] = (after(arrived[0][-1][0], joint), None)
        arrived.append(moved)

    wide, half = jnp.float32, jnp.bfloat16
    grads_q, sums, outputs_of = [], [], []
    for chunk, (head, per) in enumerate(zip(heads, CHUNKS)):
        joined = chunk < len(CHUNKS) - 1
        grad_q, *parts = attend(
            doc_lengths, queries, grad_out, lse, delta, arrived[chunk], head, per, hops, joined
        )
        grads_q.append(grad_q)
        outputs_of.append((parts[: hops + 1], parts[hops + 1 :], joined))
    before = []
    for column, crossed, joined in outputs_of:
        if joined:
            crossed = send(crossed[0], to_odd(1) + to_even(0))
            crossed = after(crossed, outputs_of[-1][1][-1])
            edge = crossed[hops - 1]
        else:
            edge = send(crossed[-1], to_odd(hops) + to_even(0))
            crossed = [
                send(after(crossed[hop - 1], *before), to_odd(hop) + to_even(hop)) for hop in range(1, hops)
            ]
        edge = edge.astype(wide)
        total = column[hops].astype(wide) + jnp.where(side == 1, edge, 0.0)
        for hop in range(hops - 1, -1, -1):
            total = total.astype(half)
            if hop == hops - 1:
                before = [total]
            far = send(total, back(hop + 1)).astype(wide)
            if hop:
                total = column[hop].astype(wide) + crossed[hop - 1].astype(wide) + far
        total = column[0] + jnp.where(side == 0, edge, 0.0) + far
        sums.append(total.astype(half))
    grads_q[-1] = after(grads_q[-1], edge)
    grad_q = jnp.concatenate(grads_q, axis=1)
    grad_keys = jnp.concatenate([total[0] for total in sums], axis=1)
    grad_values = jnp.concatenate([total[1] for total in sums], axis=1)
    return (grad_q, grad_keys, grad_values)


def solution(mesh):
    rows = P(("packs", "seq"), None)
    return jax.shard_map(
        shards,
        mesh=mesh,
        in_specs=(rows, rows, rows, rows, rows, rows, P("packs")),
        out_specs=(rows, rows, rows),
        check_vma=False,
    )
```

profile of v0, /device:TPU:0, one launch (start us, length us, event | category | flops | bytes accessed | tf_op | source)
XLA Modules:
  0.0 86.6 jit_solution(15365348829650399315)
XLA Ops:
  0.6 1.3 %slice_bitcast_fusion.4 = (bf16[1,128,512]{2,1,0:T(8,128)(2,1)S(1)}, bf16[1,128,512]{2,1,0:T(8,128)(2,1)S(1)}, bf16[1,128,512]{2,1,0:T(8,128)(2,1)S(1)}, bf16[1,128,512]{2,1,0:T(8,128)(2,1)S(1)}) fusion(bf16[128,1024]{1,0:T(8,128)(2,1)} %param.9, bf16[128,1024]{1,0:T(8,128)(2,1)} %param.8), kind=kLoop, calls=%fused_computation.27 | loop fusion | bytes 1048576 | tf_op jit(solution)/shard_map/stack | solution.py:212
  2.0 5.6 %collective-permute-start.1 = (bf16[2,128,512]{2,1,0:T(8,128)(2,1)S(1)}, bf16[2,128,512]{2,1,0:T(8,128)(2,1)}, u32[]{:S(2)}, u32[]{:S(2)}) collective-permute-start(bf16[2,128,512]{2,1,0:T(8,128)(2,1)S(1)} %pad_maximum_fusion.3.refs_0_), channel_id=1, source_target_pairs={{0,2},{1,3},{2,4},{3,5},{4,6},{5,7},{8,10},{9,11},{10,12},{11,13},... | collective-permute-start | bytes 786440 | tf_op jit(solution)/shard_map/ppermute | solution.py:201
  7.7 2.8 %collective-permute-start = (bf16[2,128,512]{2,1,0:T(8,128)(2,1)S(1)}, bf16[2,128,512]{2,1,0:T(8,128)(2,1)S(1)}, u32[]{:S(2)}, u32[]{:S(2)}) collective-permute-start(bf16[2,128,512]{2,1,0:T(8,128)(2,1)S(1)} %pad_maximum_fusion.2.refs_0_), channel_id=1, source_target_pairs={{0,2},{1,3},{2,4},{3,5},{4,6},{5,7},{8,10},{9,11},{10,12},{11,13},... | collective-permute-start | bytes 786440 | tf_op jit(solution)/shard_map/ppermute | solution.py:201
  10.5 1.6 %copy-done.1 = bf16[128,8192]{1,0:T(8,128)(2,1)S(1)} copy-done((bf16[128,8192]{1,0:T(8,128)(2,1)S(1)}, bf16[128,8192]{1,0:T(8,128)(2,1)}, u32[]{:S(2)}) %copy-start.1) | copy-done | bytes 2097176
  12.1 1.6 %copy-done.3 = bf16[128,8192]{1,0:T(8,128)(2,1)S(1)} copy-done((bf16[128,8192]{1,0:T(8,128)(2,1)S(1)}, bf16[128,8192]{1,0:T(8,128)(2,1)}, u32[]{:S(2)}) %copy-start.3) | copy-done | bytes 2097176
  13.7 1.5 %delta.1.delta_ref = f32[64,128]{1,0:T(8,128)S(1)} custom-call(bf16[128,8192]{1,0:T(8,128)(2,1)S(1)} %copy-done, bf16[128,8192]{1,0:T(8,128)(2,1)S(1)} %copy-done.3, bf16[128,8192]{1,0:T(8,128)(2,1)S(1)} %copy-done.1), custom_call_target="tpu_custom_call" | custom-call | flops 536870912 | bytes 6291456 | tf_op jit(solution)/shard_map/delta/pallas_call | solution.py:55
  16.0 1.4 %collective-permute-start.3 = (bf16[2,128,512]{2,1,0:T(8,128)(2,1)}, bf16[2,128,512]{2,1,0:T(8,128)(2,1)}, u32[]{:S(2)}, u32[]{:S(2)}) collective-permute-start(bf16[2,128,512]{2,1,0:T(8,128)(2,1)} %collective-permute-done.1.refs_1_), channel_id=1, source_target_pairs={{2,3},{4,5},{6,7},{3,2},{5,4},{7,6},{10,11},{12,13},{14,15},{11,10... | collective-permute-start | bytes 786440 | tf_op jit(solution)/shard_map/ppermute | solution.py:201
  18.8 1.0 %broadcast_select_fusion = bf16[2,128,512]{2,1,0:T(8,128)(2,1)S(1)} fusion(bf16[2,128,512]{2,1,0:T(8,128)(2,1)S(1)} %collective-permute-done.2.refs_2_, pred[]{:T(512)S(6)} %eq.4, bf16[1,128,512]{2,1,0:T(8,128)(2,1)} %copy-done.9, bf16[1,128,512]{2,1,0:T(8,128)(2,1)} %copy-done.10), kind=kLoop, calls=%fused_computation.22 | loop fusion | flops 262144 | bytes 786433 | tf_op jit(solution)/shard_map/jit(_where)/select_n | solution.py:220
  19.8 3.4 %collective-permute-start.4 = (bf16[2,128,512]{2,1,0:T(8,128)(2,1)S(1)}, bf16[2,128,512]{2,1,0:T(8,128)(2,1)S(1)}, u32[]{:S(2)}, u32[]{:S(2)}) collective-permute-start(bf16[2,128,512]{2,1,0:T(8,128)(2,1)S(1)} %broadcast_select_fusion), channel_id=1, source_target_pairs={{0,1},{2,3},{4,5},{6,7},{5,4},{7,6},{8,9},{10,11},{12,13},{14,15},... | collective-permute-start | bytes 786440 | tf_op jit(solution)/shard_map/ppermute | solution.py:201
  23.3 1.0 %select_bitcast_fusion = bf16[1,2,128,512]{3,2,1,0:T(8,128)(2,1)S(1)} fusion(bf16[2,128,512]{2,1,0:T(8,128)(2,1)S(1)} %collective-permute-done.5.refs_2_, pred[]{:T(512)S(6)} %eq.4, bf16[1,128,512]{2,1,0:T(8,128)(2,1)} %copy-done.7, bf16[1,128,512]{2,1,0:T(8,128)(2,1)} %copy-done.8), kind=kLoop, calls=%fused_computation.21 | loop fusion | flops 262144 | bytes 786433 | tf_op jit(solution)/shard_map/stack | solution.py:227
  24.3 1.3 %collective-permute-start.6 = (bf16[2,2,128,512]{3,2,1,0:T(8,128)(2,1)S(1)}, bf16[2,2,128,512]{3,2,1,0:T(8,128)(2,1)S(1)}, u32[]{:S(2)}, u32[]{:S(2)}) collective-permute-start(bf16[2,2,128,512]{3,2,1,0:T(8,128)(2,1)S(1)} %pad_maximum_fusion.1), channel_id=1, source_target_pairs={{0,1},{2,3},{4,5},{6,7},{3,2},{5,4},{7,6},{8,9},{10,11},{12,13},{1... | collective-permute-start | bytes 1572872 | tf_op jit(solution)/shard_map/ppermute | solution.py:201
  25.7 4.3 %collective-permute-done.4.refs_4_ = bf16[2,128,512]{2,1,0:T(8,128)(2,1)S(1)} collective-permute-done((bf16[2,128,512]{2,1,0:T(8,128)(2,1)S(1)}, bf16[2,128,512]{2,1,0:T(8,128)(2,1)S(1)}, u32[]{:S(2)}, u32[]{:S(2)}) %collective-permute-start.4) | collective-permute-done | bytes 262176 | tf_op jit(solution)/shard_map/ppermute | solution.py:201
  30.0 1.6 %copy-done.4 = bf16[128,8192]{1,0:T(8,128)(2,1)S(1)} copy-done((bf16[128,8192]{1,0:T(8,128)(2,1)S(1)}, bf16[128,8192]{1,0:T(8,128)(2,1)}, u32[]{:S(2)}) %copy-start.4) | copy-done | bytes 2097176
  31.6 8.5 %attend.2 = (bf16[128,4096]{1,0:T(8,128)(2,1)S(1)}, f32[2,128,512]{2,1,0:T(8,128)S(1)}, bf16[2,128,512]{2,1,0:T(8,128)(2,1)S(1)}, bf16[2,128,512]{2,1,0:T(8,128)(2,1)S(1)}, bf16[2,2,128,512]{3,2,1,0:T(8,128)(2,1)S(1)}) custom-call(s32[8]{0:T(128)S(1)} %copy-done.6, bf16[128,8192]{1,0:T(8,128)(2,1)S(1)} %copy-done.2, bf16[128,8192]{1,0:T(8,128)(2,1)S(1)} %copy-done.4, ...), custom_call_target="tpu_custom_call" | custom-call | flops 13421772800 | bytes 7077888 | tf_op jit(solution)/shard_map/attend/pallas_call | solution.py:161
  40.1 1.3 %collective-permute-start.8 = (bf16[2,2,128,512]{3,2,1,0:T(8,128)(2,1)S(1)}, bf16[2,2,128,512]{3,2,1,0:T(8,128)(2,1)S(1)}, u32[]{:S(2)}, u32[]{:S(2)}) collective-permute-start(bf16[2,2,128,512]{3,2,1,0:T(8,128)(2,1)S(1)} %get-tuple-element.34), channel_id=1, source_target_pairs={{2,3},{4,5},{6,7},{1,0},{3,2},{5,4},{7,6},{10,11},{12,13},{14,15},... | collective-permute-start | bytes 1572872 | tf_op jit(solution)/shard_map/ppermute | solution.py:201
  41.4 8.0 %attend.3 = (bf16[128,4096]{1,0:T(8,128)(2,1)S(1)}, f32[2,128,512]{2,1,0:T(8,128)S(1)}, bf16[2,128,512]{2,1,0:T(8,128)(2,1)S(1)}, bf16[2,128,512]{2,1,0:T(8,128)...) custom-call(s32[8]{0:T(128)S(1)} %copy-done.6, bf16[128,8192]{1,0:T(8,128)(2,1)S(1)} %copy-done.2, ...), custom_call_target="tpu_custom_call" | custom-call | flops 13421772800 | bytes 7077888 | tf_op jit(solution)/shard_map/attend/pallas_call | solution.py:161
  49.3 1.3 %collective-permute-start.7 = (bf16[2,128,512]{2,1,0:T(8,128)(2,1)S(1)}, bf16[2,128,512]{2,1,0:T(8,128)(2,1)S(1)}, u32[]{:S(2)}, u32[]{:S(2)}) collective-permute-start(bf16[2,128,512]{2,1,0:T(8,128)(2,1)S(1)} %get-tuple-element.31), channel_id=1, source_target_pairs={{4,5},{6,7},{1,0},{3,2},{5,4},{7,6},{12,13},{14,15},{9,8},{11,10},... | collective-permute-start | bytes 786440 | tf_op jit(solution)/shard_map/ppermute | solution.py:201
  50.6 3.1 %collective-permute-done.8 = bf16[2,2,128,512]{3,2,1,0:T(8,128)(2,1)S(1)} collective-permute-done((bf16[2,2,128,512]{3,2,1,0:T(8,128)(2,1)S(1)}, bf16[2,2,128,512]{3,2,1,0:T(8,128)(2,1)S(1)}, u32[]{:S(2)}, u32[]{:S(2)}) %collective-permute-start.8) | collective-permute-done | bytes 524320 | tf_op jit(solution)/shard_map/ppermute | solution.py:201
  55.2 2.5 %collective-permute-done.7 = bf16[2,128,512]{2,1,0:T(8,128)(2,1)S(1)} collective-permute-done((bf16[2,128,512]{2,1,0:T(8,128)(2,1)S(1)}, bf16[2,128,512]{2,1,0:T(8,128)(2,1)S(1)}, u32[]{:S(2)}, u32[]{:S(2)}) %collective-permute-start.7) | collective-permute-done | bytes 262176 | tf_op jit(solution)/shard_map/ppermute | solution.py:201
  58.5 1.3 %collective-permute-start.10 = (bf16[2,128,512]{2,1,0:T(8,128)(2,1)S(1)}, bf16[2,128,512]{2,1,0:T(8,128)(2,1)S(1)}, u32[]{:S(2)}, u32[]{:S(2)}) collective-permute-start(bf16[2,128,512]{2,1,0:T(8,128)(2,1)S(1)} %fusion.8), channel_id=1, source_target_pairs={{2,0},{3,1},{4,2},{5,3},{6,4},{7,5},{10,8},{11,9},{12,10},{13,11},... | collective-permute-start | bytes 786440 | tf_op jit(solution)/shard_map/ppermute | solution.py:201
  59.8 1.5 %pad_maximum_fusion = bf16[128,8192]{1,0:T(8,128)(2,1)} fusion(bf16[128,4096]{1,0:T(8,128)(2,1)S(1)} %get-tuple-element.32, bf16[128,4096]{1,0:T(8,128)(2,1)S(1)} %get-tuple-element.29), kind=kLoop, calls=%fused_computation | loop fusion | flops 4194304 | bytes 4194304 | tf_op jit(solution)/shard_map/concatenate | solution.py:265
  61.4 1.3 %collective-permute-start.13 = (bf16[2,128,512]{2,1,0:T(8,128)(2,1)S(1)}, bf16[2,128,512]{2,1,0:T(8,128)(2,1)S(1)}, u32[]{:S(2)}, u32[]{:S(2)}) collective-permute-start(bf16[2,128,512]{2,1,0:T(8,128)(2,1)S(1)} %add_convert_fusion.1), channel_id=1, source_target_pairs={{2,0},{3,1},{4,2},{5,3},{6,4},{7,5},{10,8},{11,9},{12,10},{13,11},... | collective-permute-start | bytes 786440 | tf_op jit(solution)/shard_map/ppermute | solution.py:201
  62.7 18.1 %collective-permute-done.10 = bf16[2,128,512]{2,1,0:T(8,128)(2,1)S(1)} collective-permute-done((bf16[2,128,512]{2,1,0:T(8,128)(2,1)S(1)}, bf16[2,128,512]{2,1,0:T(8,128)(2,1)S(1)}, u32[]{:S(2)}, u32[]{:S(2)}) %collective-permute-start.10) | collective-permute-done | bytes 262176 | tf_op jit(solution)/shard_map/ppermute | solution.py:201
  80.9 4.1 %collective-permute-done.13 = bf16[2,128,512]{2,1,0:T(8,128)(2,1)S(1)} collective-permute-done((bf16[2,128,512]{2,1,0:T(8,128)(2,1)S(1)}, bf16[2,128,512]{2,1,0:T(8,128)(2,1)S(1)}, u32[]{:S(2)}, u32[]{:S(2)}) %collective-permute-start.13) | collective-permute-done | bytes 262176 | tf_op jit(solution)/shard_map/ppermute | solution.py:201
  (46 shorter events, 6.5 us)
Async XLA Ops:
  0.6 9.9 %copy-start = (bf16[128,8192]{1,0:T(8,128)(2,1)S(1)}, bf16[128,8192]{1,0:T(8,128)(2,1)}, u32[]{:S(2)}) copy-start(bf16[128,8192]{1,0:T(8,128)(2,1)} %out_ref.1) | copy-start | bytes 6291460
  1.9 5.8 %copy-start.7 = (bf16[1,128,512]{2,1,0:T(8,128)(2,1)}, bf16[1,128,512]{2,1,0:T(8,128)(2,1)S(1)}, u32[]{:S(2)}) copy-start(bf16[1,128,512]{2,1,0:T(8,128)(2,1)S(1)} %get-tuple-element.50) | copy-start | bytes 393220
  1.9 5.7 %copy-start.8 = (bf16[1,128,512]{2,1,0:T(8,128)(2,1)}, bf16[1,128,512]{2,1,0:T(8,128)(2,1)S(1)}, u32[]{:S(2)}) copy-start(bf16[1,128,512]{2,1,0:T(8,128)(2,1)S(1)} %get-tuple-element.51) | copy-start | bytes 393220
  1.9 5.7 %copy-start.9 = (bf16[1,128,512]{2,1,0:T(8,128)(2,1)}, bf16[1,128,512]{2,1,0:T(8,128)(2,1)S(1)}, u32[]{:S(2)}) copy-start(bf16[1,128,512]{2,1,0:T(8,128)(2,1)S(1)} %get-tuple-element.49) | copy-start | bytes 393220
  2.0 5.7 %copy-start.10 = (bf16[1,128,512]{2,1,0:T(8,128)(2,1)}, bf16[1,128,512]{2,1,0:T(8,128)(2,1)S(1)}, u32[]{:S(2)}) copy-start(bf16[1,128,512]{2,1,0:T(8,128)(2,1)S(1)} %get-tuple-element.52) | copy-start | bytes 393220
  2.0 13.2 %collective-permute-start.1 = (bf16[2,128,512]{2,1,0:T(8,128)(2,1)S(1)}, bf16[2,128,512]{2,1,0:T(8,128)(2,1)}, u32[]{:S(2)}, u32[]{:S(2)}) collective-permute-start(bf16[2,128,512]{2,1,0:T(8,128)(2,1)S(1)} %pad_maximum_fusion.3.refs_0_), channel_id=1, source_target_pairs={{0,2},{1,3},{2,4},{3,5},{4,6},{5,7},{8,10},{9,11},{10,12},{11,13},... | collective-permute-start | bytes 786440 | tf_op jit(solution)/shard_map/ppermute | solution.py:201
  7.7 10.4 %collective-permute-start = (bf16[2,128,512]{2,1,0:T(8,128)(2,1)S(1)}, bf16[2,128,512]{2,1,0:T(8,128)(2,1)S(1)}, u32[]{:S(2)}, u32[]{:S(2)}) collective-permute-start(bf16[2,128,512]{2,1,0:T(8,128)(2,1)S(1)} %pad_maximum_fusion.2.refs_0_), channel_id=1, source_target_pairs={{0,2},{1,3},{2,4},{3,5},{4,6},{5,7},{8,10},{9,11},{10,12},{11,13},... | collective-permute-start | bytes 786440 | tf_op jit(solution)/shard_map/ppermute | solution.py:201
  10.5 1.6 %copy-start.1 = (bf16[128,8192]{1,0:T(8,128)(2,1)S(1)}, bf16[128,8192]{1,0:T(8,128)(2,1)}, u32[]{:S(2)}) copy-start(bf16[128,8192]{1,0:T(8,128)(2,1)} %q_ref.5) | copy-start | bytes 6291460
  15.2 14.8 %copy-start.2 = (bf16[128,8192]{1,0:T(8,128)(2,1)S(1)}, bf16[128,8192]{1,0:T(8,128)(2,1)}, u32[]{:S(2)}) copy-start(bf16[128,8192]{1,0:T(8,128)(2,1)} %q_ref.5) | copy-start | bytes 6291460
  15.2 14.8 %copy-start.5 = (f32[128,64]{0,1:T(8,128)S(1)}, f32[128,64]{0,1:T(8,128)}, u32[]{:S(2)}) copy-start(f32[128,64]{0,1:T(8,128)} %param.12) | copy-start | bytes 98308
  15.2 14.8 %copy-start.6 = (s32[8]{0:T(128)S(1)}, s32[8]{0:T(128)}, u32[]{:S(2)}) copy-start(s32[8]{0:T(128)} %docs.3) | copy-start | bytes 100
  15.2 3.6 %collective-permute-start.2 = (bf16[2,128,512]{2,1,0:T(8,128)(2,1)}, bf16[2,128,512]{2,1,0:T(8,128)(2,1)S(1)}, u32[]{:S(2)}, u32[]{:S(2)}) collective-permute-start(bf16[2,128,512]{2,1,0:T(8,128)(2,1)} %collective-permute-done.1.refs_1_), channel_id=1, source_target_pairs={{2,4},{3,5},{4,6},{5,7},{10,12},{11,13},{12,14},{13,15},{18,20},{1... | collective-permute-start | bytes 786440 | tf_op jit(solution)/shard_map/ppermute | solution.py:201
  16.0 3.8 %collective-permute-start.3 = (bf16[2,128,512]{2,1,0:T(8,128)(2,1)}, bf16[2,128,512]{2,1,0:T(8,128)(2,1)}, u32[]{:S(2)}, u32[]{:S(2)}) collective-permute-start(bf16[2,128,512]{2,1,0:T(8,128)(2,1)} %collective-permute-done.1.refs_1_), channel_id=1, source_target_pairs={{2,3},{4,5},{6,7},{3,2},{5,4},{7,6},{10,11},{12,13},{14,15},{11,10... | collective-permute-start | bytes 786440 | tf_op jit(solution)/shard_map/ppermute | solution.py:201
  18.1 5.2 %collective-permute-start.5 = (bf16[2,128,512]{2,1,0:T(8,128)(2,1)S(1)}, bf16[2,128,512]{2,1,0:T(8,128)(2,1)S(1)}, u32[]{:S(2)}, u32[]{:S(2)}) collective-permute-start(bf16[2,128,512]{2,1,0:T(8,128)(2,1)S(1)} %collective-permute-done.refs_1_), channel_id=1, source_target_pairs={{2,4},{3,5},{4,6},{5,7},{10,12},{11,13},{12,14},{13,15},{18,20},{1... | collective-permute-start | bytes 786440 | tf_op jit(solution)/shard_map/ppermute | solution.py:201
  19.8 10.2 %collective-permute-start.4 = (bf16[2,128,512]{2,1,0:T(8,128)(2,1)S(1)}, bf16[2,128,512]{2,1,0:T(8,128)(2,1)S(1)}, u32[]{:S(2)}, u32[]{:S(2)}) collective-permute-start(bf16[2,128,512]{2,1,0:T(8,128)(2,1)S(1)} %broadcast_select_fusion), channel_id=1, source_target_pairs={{0,1},{2,3},{4,5},{6,7},{5,4},{7,6},{8,9},{10,11},{12,13},{14,15},... | collective-permute-start | bytes 786440 | tf_op jit(solution)/shard_map/ppermute | solution.py:201
  24.3 17.0 %collective-permute-start.6 = (bf16[2,2,128,512]{3,2,1,0:T(8,128)(2,1)S(1)}, bf16[2,2,128,512]{3,2,1,0:T(8,128)(2,1)S(1)}, u32[]{:S(2)}, u32[]{:S(2)}) collective-permute-start(bf16[2,2,128,512]{3,2,1,0:T(8,128)(2,1)S(1)} %pad_maximum_fusion.1), channel_id=1, source_target_pairs={{0,1},{2,3},{4,5},{6,7},{3,2},{5,4},{7,6},{8,9},{10,11},{12,13},{1... | collective-permute-start | bytes 1572872 | tf_op jit(solution)/shard_map/ppermute | solution.py:201
  30.0 1.6 %copy-start.4 = (bf16[128,8192]{1,0:T(8,128)(2,1)S(1)}, bf16[128,8192]{1,0:T(8,128)(2,1)}, u32[]{:S(2)}) copy-start(bf16[128,8192]{1,0:T(8,128)(2,1)} %gout_ref.5) | copy-start | bytes 6291460
  40.1 13.7 %collective-permute-start.8 = (bf16[2,2,128,512]{3,2,1,0:T(8,128)(2,1)S(1)}, bf16[2,2,128,512]{3,2,1,0:T(8,128)(2,1)S(1)}, u32[]{:S(2)}, u32[]{:S(2)}) collective-permute-start(bf16[2,2,128,512]{3,2,1,0:T(8,128)(2,1)S(1)} %get-tuple-element.34), channel_id=1, source_target_pairs={{2,3},{4,5},{6,7},{1,0},{3,2},{5,4},{7,6},{10,11},{12,13},{14,15},... | collective-permute-start | bytes 1572872 | tf_op jit(solution)/shard_map/ppermute | solution.py:201
  49.3 8.3 %collective-permute-start.7 = (bf16[2,128,512]{2,1,0:T(8,128)(2,1)S(1)}, bf16[2,128,512]{2,1,0:T(8,128)(2,1)S(1)}, u32[]{:S(2)}, u32[]{:S(2)}) collective-permute-start(bf16[2,128,512]{2,1,0:T(8,128)(2,1)S(1)} %get-tuple-element.31), channel_id=1, source_target_pairs={{4,5},{6,7},{1,0},{3,2},{5,4},{7,6},{12,13},{14,15},{9,8},{11,10},... | collective-permute-start | bytes 786440 | tf_op jit(solution)/shard_map/ppermute | solution.py:201
  53.8 4.6 %collective-permute-start.9 = (bf16[2,128,512]{2,1,0:T(8,128)(2,1)S(1)}, bf16[2,128,512]{2,1,0:T(8,128)(2,1)S(1)}, u32[]{:S(2)}, u32[]{:S(2)}) collective-permute-start(bf16[2,128,512]{2,1,0:T(8,128)(2,1)S(1)} %fusion.6), channel_id=1, source_target_pairs={{4,2},{5,3},{6,4},{7,5},{12,10},{13,11},{14,12},{15,13},{20,18},{2... | collective-permute-start | bytes 786440 | tf_op jit(solution)/shard_map/ppermute | solution.py:201
  54.5 6.8 %collective-permute-start.11 = (bf16[2,128,512]{2,1,0:T(8,128)(2,1)S(1)}, bf16[2,128,512]{2,1,0:T(8,128)(2,1)S(1)}, u32[]{:S(2)}, u32[]{:S(2)}) collective-permute-start(bf16[2,128,512]{2,1,0:T(8,128)(2,1)S(1)} %get-tuple-element.41), channel_id=1, source_target_pairs={{2,3},{4,5},{6,7},{3,2},{5,4},{7,6},{10,11},{12,13},{14,15},{11,10... | collective-permute-start | bytes 786440 | tf_op jit(solution)/shard_map/ppermute | solution.py:201
  57.7 3.6 %collective-permute-start.12 = (bf16[2,128,512]{2,1,0:T(8,128)(2,1)S(1)}, bf16[2,128,512]{2,1,0:T(8,128)(2,1)S(1)}, u32[]{:S(2)}, u32[]{:S(2)}) collective-permute-start(bf16[2,128,512]{2,1,0:T(8,128)(2,1)S(1)} %add_convert_fusion.2), channel_id=1, source_target_pairs={{4,2},{5,3},{6,4},{7,5},{12,10},{13,11},{14,12},{15,13},{20,18},{2... | collective-permute-start | bytes 786440 | tf_op jit(solution)/shard_map/ppermute | solution.py:201
  58.5 22.3 %collective-permute-start.10 = (bf16[2,128,512]{2,1,0:T(8,128)(2,1)S(1)}, bf16[2,128,512]{2,1,0:T(8,128)(2,1)S(1)}, u32[]{:S(2)}, u32[]{:S(2)}) collective-permute-start(bf16[2,128,512]{2,1,0:T(8,128)(2,1)S(1)} %fusion.8), channel_id=1, source_target_pairs={{2,0},{3,1},{4,2},{5,3},{6,4},{7,5},{10,8},{11,9},{12,10},{13,11},... | collective-permute-start | bytes 786440 | tf_op jit(solution)/shard_map/ppermute | solution.py:201
  61.4 23.6 %collective-permute-start.13 = (bf16[2,128,512]{2,1,0:T(8,128)(2,1)S(1)}, bf16[2,128,512]{2,1,0:T(8,128)(2,1)S(1)}, u32[]{:S(2)}, u32[]{:S(2)}) collective-permute-start(bf16[2,128,512]{2,1,0:T(8,128)(2,1)S(1)} %add_convert_fusion.1), channel_id=1, source_target_pairs={{2,0},{3,1},{4,2},{5,3},{6,4},{7,5},{10,8},{11,9},{12,10},{13,11},... | collective-permute-start | bytes 786440 | tf_op jit(solution)/shard_map/ppermute | solution.py:201
  (1 other events, 1.6 us)
where the time goes:
time: 87.3 us; the launch traced here: 86.6 us
  waiting for transfers between devices  32.7 us (37%)
  starting transfers between devices  23.3 us (27%)
  Pallas kernels  17.9 us (21%)
  local copies, waits for them, and re-layouts  6.12 us (7%)
  other arithmetic  5.66 us (6%)
  between operations  0.97 us (1%)
    ppermute x14, waiting for transfers between devices, send(): return lax.ppermute(array, 'seq', pairs)  32.7 us
    ppermute x14, starting transfers between devices, send(): return lax.ppermute(array, 'seq', pairs)  23.3 us
    pallas_call x2, Pallas kernels, attend(): pl.pallas_call(functools.partial(attend_kernel, hops, joined, head, place...  16.4 us
    unnamed x22, local copies, waits for them, and re-layouts  4.8 us
  transfers between devices with their start and end apart: 14, of which 6 were waited for; matrix products, arithmetic and copies ran while one was open for 5% of the time, Pallas kernels for 21%

commit v1 on v0

--- a/solution.py
+++ b/solution.py
@@ -33,7 +33,7 @@
     )
 
 
-def delta_kernel(out_ref, gout_ref, q_ref, delta_ref):
+def delta_kernel(out_ref, gout_ref, delta_ref):
     rows = out_ref.shape[0]
     wide = GROUP * HDIM
     first = lax.broadcasted_iota(jnp.int32, (wide, HDIM), 1) * HDIM
@@ -49,22 +49,53 @@
         delta_ref[group * GROUP : (group + 1) * GROUP, :] = total.T[:GROUP]
 
 
-def delta_rows(outputs, grad_out, queries):
+def delta_rows(outputs, grad_out):
     rows = outputs.shape[0]
     local = pl.BlockSpec(memory_space=pltpu.VMEM)
     return pl.pallas_call(
         delta_kernel,
-        in_specs=[local] * 3,
+        in_specs=[local] * 2,
         out_specs=local,
         out_shape=jax.ShapeDtypeStruct((HEADS, rows), jnp.float32),
         compiler_params=pltpu.CompilerParams(vmem_limit_bytes=VMEM),
         cost_estimate=pl.CostEstimate(
             flops=4 * rows * HEADS * HDIM * HDIM,
-            bytes_accessed=6 * rows * HEADS * HDIM,
+            bytes_accessed=4 * rows * HEADS * HDIM,
             transcendentals=0,
         ),
         name="delta",
-    )(outputs, grad_out, queries)
+    )(outputs, grad_out)
+
+
+def edge_kernel(own_ref, *refs):
+    side = lax.rem(lax.axis_index("seq"), 2)
+    arrays, edge_ref = refs[:-1], refs[-1]
+    for place, array in enumerate(arrays[:-1]):
+        edge_ref[place] = array[...]
+
+    @pl.when(side == 0)
+    def _():
+        edge_ref[len(arrays) - 1] = own_ref[...]
+
+    @pl.when(side == 1)
+    def _():
+        edge_ref[len(arrays) - 1] = arrays[-1][...]
+
+
+def edge_operand(own, arrays):
+    local = pl.BlockSpec(memory_space=pltpu.VMEM)
+    shape = (len(arrays),) + own.shape
+    return pl.pallas_call(
+        edge_kernel,
+        in_specs=[local] * (1 + len(arrays)),
+        out_specs=local,
+        out_shape=jax.ShapeDtypeStruct(shape, own.dtype),
+        compiler_params=pltpu.CompilerParams(vmem_limit_bytes=VMEM),
+        cost_estimate=pl.CostEstimate(
+            flops=0, bytes_accessed=4 * len(arrays) * own.size, transcendentals=0
+        ),
+        name="edge",
+    )(own, *arrays)
 
 
 def slot_shards(me, hops):
@@ -203,7 +234,7 @@
     def after(array, *others):
         return lax.optimization_barrier((array,) + others)[0]
 
-    delta = delta_rows(outputs, grad_out, queries)
+    delta = delta_rows(outputs, grad_out)
     lse = lse_saved.T
     heads = [sum(CHUNKS[:chunk]) for chunk in range(len(CHUNKS))]
     columns = []
@@ -217,17 +248,18 @@
             column.append(send(column[-1], onward(hop)))
     arrived = []
     for chunk, column in enumerate(columns):
-        edge = jnp.where(side == 0, column[0], column[hops])
         moved = [(array, None) for array in column]
         if chunk == 0:
             crossed = [send(array, to_odd(1) + to_even(1)) for array in column[1:hops]]
-            crossed.append(send(after(edge, *crossed), to_odd(0) + to_even(hops)))
             moved += [(array, None) for array in crossed]
+            edge = edge_operand(column[0], [column[hops]])
+            edge = send(after(edge, *crossed), to_odd(0) + to_even(hops))
+            moved.append((edge, 0))
         else:
-            joint = jnp.stack(column[1:hops] + [edge])
+            joint = edge_operand(column[0], column[1:])
             crossed = send(joint, to_odd(0) + to_even(1))
             moved += [(crossed, hop) for hop in range(hops)]
-            arrived[0][-1] = (after(arrived[0][-1][0], joint), None)
+            arrived[0][-1] = (after(arrived[0][-1][0], joint), 0)
         arrived.append(moved)
 
     wide, half = jnp.float32, jnp.bfloat16

time: 87.3 us -> 98.4 us (1.13)
  local copies, waits for them, and re-layouts: 6.12 us -> 13 us
  other arithmetic: 5.66 us -> 7.47 us
  Pallas kernels: 17.9 us -> 19.2 us
    unnamed x22 -> x52, local copies, waits for them, and re-layouts: 4.8 us -> 11.7 us
    convert_element_type x4, other arithmetic: 0.37 us -> 3.3 us  [shards(): total = total.astype(half)]
    another operation x2 -> x0, other arithmetic: 1.06 us -> none  [shards(): joint = jnp.stack(column[1:hops] + [edge])]
    select_n x1 -> x0, other arithmetic: 1.01 us -> none  [shards(): edge = jnp.where(side == 0, column[0], column[hops])]
    pallas_call x1 -> x3, Pallas kernels: 1.48 us -> 2.26 us  [the longest x1 1.48 us: delta_rows(): pl.pallas_call(delta_kernel, in_specs=[local] * 2, out_specs=local, out_s...]
  transfers between devices with their start and end apart: 14 -> 14, of which waited for: 6 -> 6; matrix products, arithmetic and copies ran while one was open for 5% -> 6% of each run, Pallas kernels for 21% -> 20%
where the time goes in v1:
time: 98.4 us; the launch traced here: 97.6 us
  waiting for transfers between devices  33.5 us (34%)
  starting transfers between devices  23.5 us (24%)
  Pallas kernels  19.2 us (20%)
  local copies, waits for them, and re-layouts  13 us (13%)
  other arithmetic  7.47 us (8%)
  between operations  1 us (1%)
    ppermute x14, waiting for transfers between devices, send(): return lax.ppermute(array, 'seq', pairs)  33.5 us
    ppermute x14, starting transfers between devices, send(): return lax.ppermute(array, 'seq', pairs)  23.5 us
    pallas_call x2, Pallas kernels, attend(): pl.pallas_call(functools.partial(attend_kernel, hops, joined, head, place...  16.9 us
    unnamed x52, local copies, waits for them, and re-layouts  11.7 us
    convert_element_type x4, other arithmetic, shards(): total = total.astype(half)  3.3 us
  transfers between devices with their start and end apart: 14, of which 6 were waited for; matrix products, arithmetic and copies ran while one was open for 6% of the time, Pallas kernels for 20%

profile of v1, /device:TPU:0, one launch (start us, length us, event | category | flops | bytes accessed | tf_op | source)
XLA Modules:
  0.0 97.6 jit_solution(8610815945650914758)
XLA Ops:
  0.6 1.3 %slice_bitcast_fusion.4 = (bf16[1,128,512]{2,1,0:T(8,128)(2,1)S(1)}, bf16[1,128,512]{2,1,0:T(8,128)(2,1)S(1)}, bf16[1,128,512]{2,1,0:T(8,128)(2,1)S(1)}, bf16[1,128,512]{2,1,0:T(8,128)(2,1)S(1)}) fusion(bf16[128,1024]{1,0:T(8,128)(2,1)} %param.9, bf16[128,1024]{1,0:T(8,128)(2,1)} %param.8), kind=kLoop, calls=%fused_computation.24 | loop fusion | bytes 1048576 | tf_op jit(solution)/shard_map/stack | solution.py:243
  2.0 4.9 %collective-permute-start.1 = (bf16[2,128,512]{2,1,0:T(8,128)(2,1)S(1)}, bf16[2,128,512]{2,1,0:T(8,128)(2,1)S(1)}, u32[]{:S(2)}, u32[]{:S(2)}) collective-permute-start(bf16[2,128,512]{2,1,0:T(8,128)(2,1)S(1)} %pad_maximum_fusion.2.own_ref.refs_0_), channel_id=1, source_target_pairs={{0,2},{1,3},{2,4},{3,5},{4,6},{5,7},{8,10},{9,11},{10,12},{11,13},... | collective-permute-start | bytes 786440 | tf_op jit(solution)/shard_map/ppermute | solution.py:232
  6.9 3.5 %collective-permute-start = (bf16[2,128,512]{2,1,0:T(8,128)(2,1)S(1)}, bf16[2,128,512]{2,1,0:T(8,128)(2,1)S(1)}, u32[]{:S(2)}, u32[]{:S(2)}) collective-permute-start(bf16[2,128,512]{2,1,0:T(8,128)(2,1)S(1)} %pad_maximum_fusion.1.own_ref.refs_0_), channel_id=1, source_target_pairs={{0,2},{1,3},{2,4},{3,5},{4,6},{5,7},{8,10},{9,11},{10,12},{11,13},... | collective-permute-start | bytes 786440 | tf_op jit(solution)/shard_map/ppermute | solution.py:232
  10.5 1.6 %copy-done.1 = bf16[128,8192]{1,0:T(8,128)(2,1)S(1)} copy-done((bf16[128,8192]{1,0:T(8,128)(2,1)S(1)}, bf16[128,8192]{1,0:T(8,128)(2,1)}, u32[]{:S(2)}) %copy-start.1) | copy-done | bytes 2097176
  12.0 1.5 %delta.1.delta_ref = f32[64,128]{1,0:T(8,128)S(1)} custom-call(bf16[128,8192]{1,0:T(8,128)(2,1)S(1)} %copy-done, bf16[128,8192]{1,0:T(8,128)(2,1)S(1)} %copy-done.1), custom_call_target="tpu_custom_call" | custom-call | flops 536870912 | bytes 4194304 | tf_op jit(solution)/shard_map/delta/pallas_call | solution.py:55
  15.8 2.3 %collective-permute-done.refs_0_.refs_1_ = bf16[2,128,512]{2,1,0:T(8,128)(2,1)S(1)} collective-permute-done((bf16[2,128,512]{2,1,0:T(8,128)(2,1)S(1)}, bf16[2,128,512]{2,1,0:T(8,128)(2,1)S(1)}, u32[]{:S(2)}, u32[]{:S(2)}) %collective-permute-start) | collective-permute-done | bytes 262176 | tf_op jit(solution)/shard_map/ppermute | solution.py:232
  20.2 4.1 %collective-permute-start.4 = (bf16[1,2,128,512]{3,2,1,0:T(8,128)(2,1)}, bf16[1,2,128,512]{3,2,1,0:T(8,128)(2,1)}, u32[]{:S(2)}, u32[]{:S(2)}) collective-permute-start(bf16[1,2,128,512]{3,2,1,0:T(8,128)(2,1)} %edge.2), channel_id=1, source_target_pairs={{0,1},{2,3},{4,5},{6,7},{5,4},{7,6},{8,9},{10,11},{12,13},{14,15},... | collective-permute-start | bytes 786440 | tf_op jit(solution)/shard_map/ppermute | solution.py:232
  24.4 1.3 %collective-permute-start.6 = (bf16[2,2,128,512]{3,2,1,0:T(8,128)(2,1)S(1)}, bf16[2,2,128,512]{3,2,1,0:T(8,128)(2,1)S(1)}, u32[]{:S(2)}, u32[]{:S(2)}) collective-permute-start(bf16[2,2,128,512]{3,2,1,0:T(8,128)(2,1)S(1)} %edge.3), channel_id=1, source_target_pairs={{0,1},{2,3},{4,5},{6,7},{3,2},{5,4},{7,6},{8,9},{10,11},{12,13},{1... | collective-permute-start | bytes 1572872 | tf_op jit(solution)/shard_map/ppermute | solution.py:232
  25.7 5.0 %collective-permute-done.4.refs_4_ = bf16[1,2,128,512]{3,2,1,0:T(8,128)(2,1)} collective-permute-done((bf16[1,2,128,512]{3,2,1,0:T(8,128)(2,1)}, bf16[1,2,128,512]{3,2,1,0:T(8,128)(2,1)}, u32[]{:S(2)}, u32[]{:S(2)}) %collective-permute-start.4) | collective-permute-done | bytes 262176 | tf_op jit(solution)/shard_map/ppermute | solution.py:232
  30.7 1.6 %copy-done.17 = bf16[128,8192]{1,0:T(8,128)(2,1)S(1)} copy-done((bf16[128,8192]{1,0:T(8,128)(2,1)S(1)}, bf16[128,8192]{1,0:T(8,128)(2,1)}, u32[]{:S(2)}) %copy-start.17) | copy-done | bytes 2097176
  34.2 8.5 %attend.2 = (bf16[128,4096]{1,0:T(8,128)(2,1)S(1)}, f32[2,128,512]{2,1,0:T(8,128)S(1)}, bf16[2,128,512]{2,1,0:T(8,128)(2,1)S(1)}, bf16[2,128,512]{2,1,0:T(8,128)(2,1)S(1)}, bf16[2,2,128,512]{3,2,1,0:T(8,128)(2,1)S(1)}) custom-call(s32[8]{0:T(128)S(1)} %copy-done.25, bf16[128,8192]{1,0:T(8,128)(2,1)S(1)} %copy-done.17, bf16[128,8192]{1,0:T(8,128)(2,1)S(1)} %copy-done.2, ...), custom_call_target="tpu_custom_call" | custom-call | flops 13421772800 | bytes 7077888 | tf_op jit(solution)/shard_map/attend/pallas_call | solution.py:192
  44.5 1.3 %collective-permute-start.8 = (bf16[2,2,128,512]{3,2,1,0:T(8,128)(2,1)S(1)}, bf16[2,2,128,512]{3,2,1,0:T(8,128)(2,1)}, u32[]{:S(2)}, u32[]{:S(2)}) collective-permute-start(bf16[2,2,128,512]{3,2,1,0:T(8,128)(2,1)S(1)} %get-tuple-element.34), channel_id=1, source_target_pairs={{2,3},{4,5},{6,7},{1,0},{3,2},{5,4},{7,6},{10,11},{12,13},{14,15},... | collective-permute-start | bytes 1572872 | tf_op jit(solution)/shard_map/ppermute | solution.py:232
  47.7 8.4 %attend.3 = (bf16[128,4096]{1,0:T(8,128)(2,1)S(1)}, f32[2,128,512]{2,1,0:T(8,128)S(1)}, bf16[2,128,512]{2,1,0:T(8,128)(2,1)S(1)}, bf16[2,128,512]{2,1,0:T(8,128)...) custom-call(s32[8]{0:T(128)S(1)} %copy-done.25, bf16[128,8192]{1,0:T(8,128)(2,1)S(1)} %copy-done.18, ...), custom_call_target="tpu_custom_call" | custom-call | flops 13421772800 | bytes 7077888 | tf_op jit(solution)/shard_map/attend/pallas_call | solution.py:192
  57.6 1.4 %collective-permute-start.7 = (bf16[2,128,512]{2,1,0:T(8,128)(2,1)}, bf16[2,128,512]{2,1,0:T(8,128)(2,1)S(1)}, u32[]{:S(2)}, u32[]{:S(2)}) collective-permute-start(bf16[2,128,512]{2,1,0:T(8,128)(2,1)} %get-tuple-element.31), channel_id=1, source_target_pairs={{4,5},{6,7},{1,0},{3,2},{5,4},{7,6},{12,13},{14,15},{9,8},{11,10},... | collective-permute-start | bytes 786440 | tf_op jit(solution)/shard_map/ppermute | solution.py:232
  59.1 1.0 %fusion.6 = bf16[2,128,512]{2,1,0:T(8,128)(2,1)S(1)} fusion(bf16[2,128,512]{2,1,0:T(8,128)(2,1)S(1)} %get-tuple-element.37, pred[]{:T(512)S(6)} %eq.9, bf16[2,2,128,512]{3,2,1,0:T(8,128)(2,1)} %collective-permute-done.8), kind=kLoop, calls=%fused_computation.9 | loop fusion | flops 655360 | bytes 786433 | tf_op jit(solution)/shard_map/convert_element_type | solution.py:288
  61.5 5.5 %collective-permute-done.7 = bf16[2,128,512]{2,1,0:T(8,128)(2,1)S(1)} collective-permute-done((bf16[2,128,512]{2,1,0:T(8,128)(2,1)}, bf16[2,128,512]{2,1,0:T(8,128)(2,1)S(1)}, u32[]{:S(2)}, u32[]{:S(2)}) %collective-permute-start.7) | collective-permute-done | bytes 262176 | tf_op jit(solution)/shard_map/ppermute | solution.py:232
  67.0 1.0 %add_convert_fusion.2 = bf16[2,128,512]{2,1,0:T(8,128)(2,1)S(1)} fusion(bf16[2,128,512]{2,1,0:T(8,128)(2,1)} %copy-done.16, bf16[2,128,512]{2,1,0:T(8,128)(2,1)S(1)} %collective-permute-done.7, pred[]{:T(512)S(6)} %eq.9), kind=kLoop, calls=%fused_computation.15 | loop fusion | flops 655360 | bytes 786433 | tf_op jit(solution)/shard_map/convert_element_type | solution.py:288
  68.8 1.1 %fusion.8 = bf16[2,128,512]{2,1,0:T(8,128)(2,1)S(1)} fusion(bf16[2,128,512]{2,1,0:T(8,128)(2,1)S(1)} %collective-permute-done.9, bf16[2,128,512]{2,1,0:T(8,128)(2,1)} %copy-done.13, bf16[2,2,128,512]{3,2,1,0:T(8,128)(2,1)} %collective-permute-done.8), kind=kLoop, calls=%fused_computation.12 | loop fusion | flops 786432 | bytes 1048576 | tf_op jit(solution)/shard_map/convert_element_type | solution.py:288
  69.9 1.3 %collective-permute-start.10 = (bf16[2,128,512]{2,1,0:T(8,128)(2,1)S(1)}, bf16[2,128,512]{2,1,0:T(8,128)(2,1)S(1)}, u32[]{:S(2)}, u32[]{:S(2)}) collective-permute-start(bf16[2,128,512]{2,1,0:T(8,128)(2,1)S(1)} %fusion.8), channel_id=1, source_target_pairs={{2,0},{3,1},{4,2},{5,3},{6,4},{7,5},{10,8},{11,9},{12,10},{13,11},... | collective-permute-start | bytes 786440 | tf_op jit(solution)/shard_map/ppermute | solution.py:232
  71.2 1.5 %pad_maximum_fusion = bf16[128,8192]{1,0:T(8,128)(2,1)} fusion(bf16[128,4096]{1,0:T(8,128)(2,1)S(1)} %get-tuple-element.32, bf16[128,4096]{1,0:T(8,128)(2,1)S(1)} %copy-done.4), kind=kLoop, calls=%fused_computation | loop fusion | flops 4194304 | bytes 4194304 | tf_op jit(solution)/shard_map/concatenate | solution.py:297
  72.8 1.4 %collective-permute-start.13 = (bf16[2,128,512]{2,1,0:T(8,128)(2,1)S(1)}, bf16[2,128,512]{2,1,0:T(8,128)(2,1)S(1)}, u32[]{:S(2)}, u32[]{:S(2)}) collective-permute-start(bf16[2,128,512]{2,1,0:T(8,128)(2,1)S(1)} %add_convert_fusion.1), channel_id=1, source_target_pairs={{2,0},{3,1},{4,2},{5,3},{6,4},{7,5},{10,8},{11,9},{12,10},{13,11},... | collective-permute-start | bytes 786440 | tf_op jit(solution)/shard_map/ppermute | solution.py:232
  74.2 16.3 %collective-permute-done.10 = bf16[2,128,512]{2,1,0:T(8,128)(2,1)S(1)} collective-permute-done((bf16[2,128,512]{2,1,0:T(8,128)(2,1)S(1)}, bf16[2,128,512]{2,1,0:T(8,128)(2,1)S(1)}, u32[]{:S(2)}, u32[]{:S(2)}) %collective-permute-start.10) | collective-permute-done | bytes 262176 | tf_op jit(solution)/shard_map/ppermute | solution.py:232
  90.5 1.1 %fusion.3 = bf16[2,128,512]{2,1,0:T(8,128)(2,1)S(1)} fusion(f32[2,128,512]{2,1,0:T(8,128)S(1)} %copy-done.6, bf16[2,128,512]{2,1,0:T(8,128)(2,1)S(1)} %collective-permute-done.10, pred[]{:T(512)S(6)} %eq.8, bf16[2,2,128,512]{3,2,1,0:T(8,128)(2,1)} %collective-permute-done.8), kind=kLoop, calls=%fused_computation.6 | loop fusion | flops 786432 | bytes 1310721 | tf_op jit(solution)/shard_map/convert_element_type | solution.py:295
  91.6 4.3 %collective-permute-done.13 = bf16[2,128,512]{2,1,0:T(8,128)(2,1)S(1)} collective-permute-done((bf16[2,128,512]{2,1,0:T(8,128)(2,1)S(1)}, bf16[2,128,512]{2,1,0:T(8,128)(2,1)S(1)}, u32[]{:S(2)}, u32[]{:S(2)}) %collective-permute-start.13) | collective-permute-done | bytes 262176 | tf_op jit(solution)/shard_map/ppermute | solution.py:232
  (75 shorter events, 15.3 us)
Async XLA Ops:
  0.6 9.8 %copy-start = (bf16[128,8192]{1,0:T(8,128)(2,1)S(1)}, bf16[128,8192]{1,0:T(8,128)(2,1)}, u32[]{:S(2)}) copy-start(bf16[128,8192]{1,0:T(8,128)(2,1)} %out_ref.1) | copy-start | bytes 6291460
  2.0 11.6 %collective-permute-start.1 = (bf16[2,128,512]{2,1,0:T(8,128)(2,1)S(1)}, bf16[2,128,512]{2,1,0:T(8,128)(2,1)S(1)}, u32[]{:S(2)}, u32[]{:S(2)}) collective-permute-start(bf16[2,128,512]{2,1,0:T(8,128)(2,1)S(1)} %pad_maximum_fusion.2.own_ref.refs_0_), channel_id=1, source_target_pairs={{0,2},{1,3},{2,4},{3,5},{4,6},{5,7},{8,10},{9,11},{10,12},{11,13},... | collective-permute-start | bytes 786440 | tf_op jit(solution)/shard_map/ppermute | solution.py:232
  6.9 11.1 %collective-permute-start = (bf16[2,128,512]{2,1,0:T(8,128)(2,1)S(1)}, bf16[2,128,512]{2,1,0:T(8,128)(2,1)S(1)}, u32[]{:S(2)}, u32[]{:S(2)}) collective-permute-start(bf16[2,128,512]{2,1,0:T(8,128)(2,1)S(1)} %pad_maximum_fusion.1.own_ref.refs_0_), channel_id=1, source_target_pairs={{0,2},{1,3},{2,4},{3,5},{4,6},{5,7},{8,10},{9,11},{10,12},{11,13},... | collective-permute-start | bytes 786440 | tf_op jit(solution)/shard_map/ppermute | solution.py:232
  12.0 18.6 %copy-start.24 = (f32[128,64]{0,1:T(8,128)S(1)}, f32[128,64]{0,1:T(8,128)}, u32[]{:S(2)}) copy-start(f32[128,64]{0,1:T(8,128)} %param.12) | copy-start | bytes 98308
  13.5 17.1 %copy-start.2 = (bf16[128,8192]{1,0:T(8,128)(2,1)S(1)}, bf16[128,8192]{1,0:T(8,128)(2,1)}, u32[]{:S(2)}) copy-start(bf16[128,8192]{1,0:T(8,128)(2,1)} %gout_ref.5) | copy-start | bytes 6291460
  13.5 17.1 %copy-start.25 = (s32[8]{0:T(128)S(1)}, s32[8]{0:T(128)}, u32[]{:S(2)}) copy-start(s32[8]{0:T(128)} %docs.3) | copy-start | bytes 100
  13.6 5.1 %collective-permute-start.2 = (bf16[2,128,512]{2,1,0:T(8,128)(2,1)S(1)}, bf16[2,128,512]{2,1,0:T(8,128)(2,1)S(1)}, u32[]{:S(2)}, u32[]{:S(2)}) collective-permute-start(bf16[2,128,512]{2,1,0:T(8,128)(2,1)S(1)} %collective-permute-done.1.refs_1_), channel_id=1, source_target_pairs={{2,4},{3,5},{4,6},{5,7},{10,12},{11,13},{12,14},{13,15},{18,20},{1... | collective-permute-start | bytes 786440 | tf_op jit(solution)/shard_map/ppermute | solution.py:232
  14.4 5.1 %collective-permute-start.3 = (bf16[2,128,512]{2,1,0:T(8,128)(2,1)S(1)}, bf16[2,128,512]{2,1,0:T(8,128)(2,1)S(1)}, u32[]{:S(2)}, u32[]{:S(2)}) collective-permute-start(bf16[2,128,512]{2,1,0:T(8,128)(2,1)S(1)} %collective-permute-done.1.refs_1_), channel_id=1, source_target_pairs={{2,3},{4,5},{6,7},{3,2},{5,4},{7,6},{10,11},{12,13},{14,15},{11,10... | collective-permute-start | bytes 786440 | tf_op jit(solution)/shard_map/ppermute | solution.py:232
  18.1 24.7 %copy-start.9 = (bf16[2,128,512]{2,1,0:T(8,128)(2,1)}, bf16[2,128,512]{2,1,0:T(8,128)(2,1)S(1)}, u32[]{:S(2)}) copy-start(bf16[2,128,512]{2,1,0:T(8,128)(2,1)S(1)} %collective-permute-done.refs_0_.refs_1_) | copy-start | bytes 786436
  18.1 6.3 %collective-permute-start.5 = (bf16[2,128,512]{2,1,0:T(8,128)(2,1)S(1)}, bf16[2,128,512]{2,1,0:T(8,128)(2,1)S(1)}, u32[]{:S(2)}, u32[]{:S(2)}) collective-permute-start(bf16[2,128,512]{2,1,0:T(8,128)(2,1)S(1)} %collective-permute-done.refs_0_.refs_1_), channel_id=1, source_target_pairs={{2,4},{3,5},{4,6},{5,7},{10,12},{11,13},{12,14},{13,15},{18,20},{1... | collective-permute-start | bytes 786440 | tf_op jit(solution)/shard_map/ppermute | solution.py:232
  20.2 10.5 %collective-permute-start.4 = (bf16[1,2,128,512]{3,2,1,0:T(8,128)(2,1)}, bf16[1,2,128,512]{3,2,1,0:T(8,128)(2,1)}, u32[]{:S(2)}, u32[]{:S(2)}) collective-permute-start(bf16[1,2,128,512]{3,2,1,0:T(8,128)(2,1)} %edge.2), channel_id=1, source_target_pairs={{0,1},{2,3},{4,5},{6,7},{5,4},{7,6},{8,9},{10,11},{12,13},{14,15},... | collective-permute-start | bytes 786440 | tf_op jit(solution)/shard_map/ppermute | solution.py:232
  24.3 18.4 %copy-start.11 = (bf16[2,128,512]{2,1,0:T(8,128)(2,1)}, bf16[2,128,512]{2,1,0:T(8,128)(2,1)S(1)}, u32[]{:S(2)}) copy-start(bf16[2,128,512]{2,1,0:T(8,128)(2,1)S(1)} %collective-permute-done.5.refs_1_.refs_2_) | copy-start | bytes 786436
  24.4 21.4 %collective-permute-start.6 = (bf16[2,2,128,512]{3,2,1,0:T(8,128)(2,1)S(1)}, bf16[2,2,128,512]{3,2,1,0:T(8,128)(2,1)S(1)}, u32[]{:S(2)}, u32[]{:S(2)}) collective-permute-start(bf16[2,2,128,512]{3,2,1,0:T(8,128)(2,1)S(1)} %edge.3), channel_id=1, source_target_pairs={{0,1},{2,3},{4,5},{6,7},{3,2},{5,4},{7,6},{8,9},{10,11},{12,13},{1... | collective-permute-start | bytes 1572872 | tf_op jit(solution)/shard_map/ppermute | solution.py:232
  34.2 11.6 %copy-start.18 = (bf16[128,8192]{1,0:T(8,128)(2,1)S(1)}, bf16[128,8192]{1,0:T(8,128)(2,1)}, u32[]{:S(2)}) copy-start(bf16[128,8192]{1,0:T(8,128)(2,1)} %q_ref.3) | copy-start | bytes 6291460
  44.5 14.6 %collective-permute-start.8 = (bf16[2,2,128,512]{3,2,1,0:T(8,128)(2,1)S(1)}, bf16[2,2,128,512]{3,2,1,0:T(8,128)(2,1)}, u32[]{:S(2)}, u32[]{:S(2)}) collective-permute-start(bf16[2,2,128,512]{3,2,1,0:T(8,128)(2,1)S(1)} %get-tuple-element.34), channel_id=1, source_target_pairs={{2,3},{4,5},{6,7},{1,0},{3,2},{5,4},{7,6},{10,11},{12,13},{14,15},... | collective-permute-start | bytes 1572872 | tf_op jit(solution)/shard_map/ppermute | solution.py:232
  57.6 13.5 %copy-start.4 = (bf16[128,4096]{1,0:T(8,128)(2,1)S(1)}, bf16[128,4096]{1,0:T(8,128)(2,1)}, u32[]{:S(2)}) copy-start(bf16[128,4096]{1,0:T(8,128)(2,1)} %copy-done.3) | copy-start | bytes 3145732
  57.6 9.4 %collective-permute-start.7 = (bf16[2,128,512]{2,1,0:T(8,128)(2,1)}, bf16[2,128,512]{2,1,0:T(8,128)(2,1)S(1)}, u32[]{:S(2)}, u32[]{:S(2)}) collective-permute-start(bf16[2,128,512]{2,1,0:T(8,128)(2,1)} %get-tuple-element.31), channel_id=1, source_target_pairs={{4,5},{6,7},{1,0},{3,2},{5,4},{7,6},{12,13},{14,15},{9,8},{11,10},... | collective-permute-start | bytes 786440 | tf_op jit(solution)/shard_map/ppermute | solution.py:232
  60.1 8.6 %collective-permute-start.9 = (bf16[2,128,512]{2,1,0:T(8,128)(2,1)S(1)}, bf16[2,128,512]{2,1,0:T(8,128)(2,1)S(1)}, u32[]{:S(2)}, u32[]{:S(2)}) collective-permute-start(bf16[2,128,512]{2,1,0:T(8,128)(2,1)S(1)} %fusion.6), channel_id=1, source_target_pairs={{4,2},{5,3},{6,4},{7,5},{12,10},{13,11},{14,12},{15,13},{20,18},{2... | collective-permute-start | bytes 786440 | tf_op jit(solution)/shard_map/ppermute | solution.py:232
  60.8 11.9 %collective-permute-start.11 = (bf16[2,128,512]{2,1,0:T(8,128)(2,1)}, bf16[2,128,512]{2,1,0:T(8,128)(2,1)S(1)}, u32[]{:S(2)}, u32[]{:S(2)}) collective-permute-start(bf16[2,128,512]{2,1,0:T(8,128)(2,1)} %copy-done.23), channel_id=1, source_target_pairs={{2,3},{4,5},{6,7},{3,2},{5,4},{7,6},{10,11},{12,13},{14,15},{11,10... | collective-permute-start | bytes 786440 | tf_op jit(solution)/shard_map/ppermute | solution.py:232
  68.1 4.6 %collective-permute-start.12 = (bf16[2,128,512]{2,1,0:T(8,128)(2,1)S(1)}, bf16[2,128,512]{2,1,0:T(8,128)(2,1)S(1)}, u32[]{:S(2)}, u32[]{:S(2)}) collective-permute-start(bf16[2,128,512]{2,1,0:T(8,128)(2,1)S(1)} %add_convert_fusion.2), channel_id=1, source_target_pairs={{4,2},{5,3},{6,4},{7,5},{12,10},{13,11},{14,12},{15,13},{20,18},{2... | collective-permute-start | bytes 786440 | tf_op jit(solution)/shard_map/ppermute | solution.py:232
  69.9 20.6 %collective-permute-start.10 = (bf16[2,128,512]{2,1,0:T(8,128)(2,1)S(1)}, bf16[2,128,512]{2,1,0:T(8,128)(2,1)S(1)}, u32[]{:S(2)}, u32[]{:S(2)}) collective-permute-start(bf16[2,128,512]{2,1,0:T(8,128)(2,1)S(1)} %fusion.8), channel_id=1, source_target_pairs={{2,0},{3,1},{4,2},{5,3},{6,4},{7,5},{10,8},{11,9},{12,10},{13,11},... | collective-permute-start | bytes 786440 | tf_op jit(solution)/shard_map/ppermute | solution.py:232
  71.2 19.3 %copy-start.6 = (f32[2,128,512]{2,1,0:T(8,128)S(1)}, f32[2,128,512]{2,1,0:T(8,128)}, u32[]{:S(2)}) copy-start(f32[2,128,512]{2,1,0:T(8,128)} %copy-done.5) | copy-start | bytes 1572868
  72.7 23.3 %copy-start.8 = (f32[2,128,512]{2,1,0:T(8,128)S(1)}, f32[2,128,512]{2,1,0:T(8,128)}, u32[]{:S(2)}) copy-start(f32[2,128,512]{2,1,0:T(8,128)} %copy-done.7) | copy-start | bytes 1572868
  72.8 23.2 %collective-permute-start.13 = (bf16[2,128,512]{2,1,0:T(8,128)(2,1)S(1)}, bf16[2,128,512]{2,1,0:T(8,128)(2,1)S(1)}, u32[]{:S(2)}, u32[]{:S(2)}) collective-permute-start(bf16[2,128,512]{2,1,0:T(8,128)(2,1)S(1)} %add_convert_fusion.1), channel_id=1, source_target_pairs={{2,0},{3,1},{4,2},{5,3},{6,4},{7,5},{10,8},{11,9},{12,10},{13,11},... | collective-permute-start | bytes 786440 | tf_op jit(solution)/shard_map/ppermute | solution.py:232
  (16 other events, 19.4 us)

commit v2 on v0

--- a/solution.py
+++ b/solution.py
@@ -180,6 +180,40 @@
     )(*operands)
 
 
+def finish_kernel(chunks, *refs):
+    key_ref, value_ref = refs[-2:]
+    refs = refs[:-2]
+    keep = jnp.where(lax.rem(lax.axis_index("seq"), 2) == 0, 1.0, 0.0)
+    for start, done in chunks:
+        if done:
+            total, refs = refs[0][...], refs[1:]
+        else:
+            own, edge, far = (ref[...].astype(jnp.float32) for ref in refs[:3])
+            total, refs = (own + edge * keep + far).astype(jnp.bfloat16), refs[3:]
+        key_ref[:, start : start + total.shape[2]] = total[0]
+        value_ref[:, start : start + total.shape[2]] = total[1]
+
+
+def finish(sums, shape):
+    operands, chunks, start = [], [], 0
+    for part in sums:
+        chunks.append((start, len(part) == 1))
+        start += part[0].shape[2]
+        operands += part
+    local = pl.BlockSpec(memory_space=pltpu.VMEM)
+    return pl.pallas_call(
+        functools.partial(finish_kernel, chunks),
+        in_specs=[local] * len(operands),
+        out_specs=[local] * 2,
+        out_shape=[jax.ShapeDtypeStruct(shape, jnp.bfloat16)] * 2,
+        compiler_params=pltpu.CompilerParams(vmem_limit_bytes=VMEM),
+        cost_estimate=pl.CostEstimate(
+            flops=8 * shape[0] * shape[1], bytes_accessed=16 * shape[0] * shape[1], transcendentals=0
+        ),
+        name="finish",
+    )(*operands)
+
+
 def shards(queries, keys, values, outputs, grad_out, lse_saved, doc_lengths):
     seq = lax.axis_size("seq")
     me = lax.axis_index("seq").astype(jnp.int32)
@@ -209,7 +243,7 @@
     columns = []
     for head, per in zip(heads, CHUNKS):
         at = slice(head * HDIM, (head + per) * HDIM)
-        own = jnp.stack([keys[:, at], values[:, at]])
+        own = lax.optimization_barrier(jnp.stack([keys[:, at], values[:, at]]))
         columns.append([own, send(own, onward(1))])
         columns[-1][1], delta = lax.optimization_barrier((columns[-1][1], delta))
     for column in columns:
@@ -248,23 +282,27 @@
         else:
             edge = send(crossed[-1], to_odd(hops) + to_even(0))
             crossed = [
-                send(after(crossed[hop - 1], *before), to_odd(hop) + to_even(hop)) for hop in range(1, hops)
+                send(after(crossed[hop - 1], before[0]), to_odd(hop) + to_even(hop)) for hop in range(1, hops)
             ]
         edge = edge.astype(wide)
         total = column[hops].astype(wide) + jnp.where(side == 1, edge, 0.0)
         for hop in range(hops - 1, -1, -1):
             total = total.astype(half)
-            if hop == hops - 1:
-                before = [total]
+            if joined:
+                before.append(total)
+            elif hop == 0:
+                total = after(total, *before)
             far = send(total, back(hop + 1)).astype(wide)
             if hop:
                 total = column[hop].astype(wide) + crossed[hop - 1].astype(wide) + far
-        total = column[0] + jnp.where(side == 0, edge, 0.0) + far
-        sums.append(total.astype(half))
+        if joined:
+            total = column[0] + jnp.where(side == 0, edge, 0.0) + far
+            sums.append([total.astype(half)])
+        else:
+            sums.append([column[0], edge.astype(half), far.astype(half)])
     grads_q[-1] = after(grads_q[-1], edge)
     grad_q = jnp.concatenate(grads_q, axis=1)
-    grad_keys = jnp.concatenate([total[0] for total in sums], axis=1)
-    grad_values = jnp.concatenate([total[1] for total in sums], axis=1)
+    grad_keys, grad_values = finish(sums, keys.shape)
     return (grad_q, grad_keys, grad_values)
 
 

time: 87.3 us -> 96.2 us (1.10)
  local copies, waits for them, and re-layouts: 6.12 us -> 12.7 us
  Pallas kernels: 17.9 us -> 19.7 us
    unnamed x22 -> x46, local copies, waits for them, and re-layouts: 4.8 us -> 11.4 us
    convert_element_type x4, other arithmetic: 0.37 us -> 3.38 us  [shards(): total = total.astype(half)]
    concatenate x2 -> x0, other arithmetic: 1.46 us -> none  [the longest x1 0.73 us: shards(): grad_values = jnp.concatenate([total[1] for total in sums], axis=1)]
    pallas_call x2, Pallas kernels: 16.4 us -> 17.4 us  [attend(): pl.pallas_call(functools.partial(attend_kernel, hops, joined, head, place...]
    another operation x2, other arithmetic: 1.06 us -> 0.08 us  [shards(): joint = jnp.stack(column[1:hops] + [edge])]
    select_n x1, other arithmetic: 1.01 us -> 0.03 us  [shards(): edge = jnp.where(side == 0, column[0], column[hops])]
  transfers between devices with their start and end apart: 14 -> 14, of which waited for: 6 -> 5; matrix products, arithmetic and copies ran while one was open for 5% -> 6% of each run, Pallas kernels for 21% -> 20%
where the time goes in v2:
time: 96.2 us; the launch traced here: 95.5 us
  waiting for transfers between devices  32.6 us (34%)
  starting transfers between devices  23.4 us (24%)
  Pallas kernels  19.7 us (20%)
  local copies, waits for them, and re-layouts  12.7 us (13%)
  other arithmetic  6.08 us (6%)
  between operations  0.98 us (1%)
    ppermute x14, waiting for transfers between devices, send(): return lax.ppermute(array, 'seq', pairs)  32.6 us
    ppermute x14, starting transfers between devices, send(): return lax.ppermute(array, 'seq', pairs)  23.4 us
    pallas_call x2, Pallas kernels, attend(): pl.pallas_call(functools.partial(attend_kernel, hops, joined, head, place...  17.4 us
    unnamed x46, local copies, waits for them, and re-layouts  11.4 us
    convert_element_type x4, other arithmetic, shards(): total = total.astype(half)  3.38 us
  transfers between devices with their start and end apart: 14, of which 5 were waited for; matrix products, arithmetic and copies ran while one was open for 6% of the time, Pallas kernels for 20%

profile of v2, /device:TPU:0, one launch (start us, length us, event | category | flops | bytes accessed | tf_op | source)
XLA Modules:
  0.0 95.5 jit_solution(3931416766757862811)
XLA Ops:
  0.6 1.3 %slice_bitcast_fusion = (bf16[1,128,512]{2,1,0:T(8,128)(2,1)S(1)}, bf16[1,128,512]{2,1,0:T(8,128)(2,1)S(1)}, bf16[1,128,512]{2,1,0:T(8,128)(2,1)S(1)}, bf16[1,128,512]{2,1,0:T(8,128)(2,1)S(1)}) fusion(bf16[128,1024]{1,0:T(8,128)(2,1)} %param.9, bf16[128,1024]{1,0:T(8,128)(2,1)} %param.8), kind=kLoop, calls=%fused_computation.20 | loop fusion | bytes 1048576 | tf_op jit(solution)/shard_map/stack | solution.py:246
  2.0 5.6 %collective-permute-start.1 = (bf16[2,128,512]{2,1,0:T(8,128)(2,1)S(1)}, bf16[2,128,512]{2,1,0:T(8,128)(2,1)}, u32[]{:S(2)}, u32[]{:S(2)}) collective-permute-start(bf16[2,128,512]{2,1,0:T(8,128)(2,1)S(1)} %pad_maximum_fusion.3.refs_0_), channel_id=1, source_target_pairs={{0,2},{1,3},{2,4},{3,5},{4,6},{5,7},{8,10},{9,11},{10,12},{11,13},... | collective-permute-start | bytes 786440 | tf_op jit(solution)/shard_map/ppermute | solution.py:235
  7.6 2.8 %collective-permute-start = (bf16[2,128,512]{2,1,0:T(8,128)(2,1)S(1)}, bf16[2,128,512]{2,1,0:T(8,128)(2,1)S(1)}, u32[]{:S(2)}, u32[]{:S(2)}) collective-permute-start(bf16[2,128,512]{2,1,0:T(8,128)(2,1)S(1)} %pad_maximum_fusion.2.refs_0_), channel_id=1, source_target_pairs={{0,2},{1,3},{2,4},{3,5},{4,6},{5,7},{8,10},{9,11},{10,12},{11,13},... | collective-permute-start | bytes 786440 | tf_op jit(solution)/shard_map/ppermute | solution.py:235
  10.5 1.6 %copy-done.1 = bf16[128,8192]{1,0:T(8,128)(2,1)S(1)} copy-done((bf16[128,8192]{1,0:T(8,128)(2,1)S(1)}, bf16[128,8192]{1,0:T(8,128)(2,1)}, u32[]{:S(2)}) %copy-start.1) | copy-done | bytes 2097176
  12.0 1.6 %copy-done.3 = bf16[128,8192]{1,0:T(8,128)(2,1)S(1)} copy-done((bf16[128,8192]{1,0:T(8,128)(2,1)S(1)}, bf16[128,8192]{1,0:T(8,128)(2,1)}, u32[]{:S(2)}) %copy-start.3) | copy-done | bytes 2097176
  13.6 1.5 %delta.1.delta_ref = f32[64,128]{1,0:T(8,128)S(1)} custom-call(bf16[128,8192]{1,0:T(8,128)(2,1)S(1)} %copy-done, bf16[128,8192]{1,0:T(8,128)(2,1)S(1)} %copy-done.3, bf16[128,8192]{1,0:T(8,128)(2,1)S(1)} %copy-done.1), custom_call_target="tpu_custom_call" | custom-call | flops 536870912 | bytes 6291456 | tf_op jit(solution)/shard_map/delta/pallas_call | solution.py:55
  15.9 1.4 %collective-permute-start.3 = (bf16[2,128,512]{2,1,0:T(8,128)(2,1)}, bf16[2,128,512]{2,1,0:T(8,128)(2,1)}, u32[]{:S(2)}, u32[]{:S(2)}) collective-permute-start(bf16[2,128,512]{2,1,0:T(8,128)(2,1)} %collective-permute-done.1.refs_1_), channel_id=1, source_target_pairs={{2,3},{4,5},{6,7},{3,2},{5,4},{7,6},{10,11},{12,13},{14,15},{11,10... | collective-permute-start | bytes 786440 | tf_op jit(solution)/shard_map/ppermute | solution.py:235
  18.8 3.5 %collective-permute-start.4 = (bf16[2,128,512]{2,1,0:T(8,128)(2,1)S(1)}, bf16[2,128,512]{2,1,0:T(8,128)(2,1)S(1)}, u32[]{:S(2)}, u32[]{:S(2)}) collective-permute-start(bf16[2,128,512]{2,1,0:T(8,128)(2,1)S(1)} %broadcast_select_fusion), channel_id=1, source_target_pairs={{0,1},{2,3},{4,5},{6,7},{5,4},{7,6},{8,9},{10,11},{12,13},{14,15},... | collective-permute-start | bytes 786440 | tf_op jit(solution)/shard_map/ppermute | solution.py:235
  22.4 1.3 %collective-permute-start.6 = (bf16[2,2,128,512]{3,2,1,0:T(8,128)(2,1)S(1)}, bf16[2,2,128,512]{3,2,1,0:T(8,128)(2,1)S(1)}, u32[]{:S(2)}, u32[]{:S(2)}) collective-permute-start(bf16[2,2,128,512]{3,2,1,0:T(8,128)(2,1)S(1)} %pad_maximum_fusion.1), channel_id=1, source_target_pairs={{0,1},{2,3},{4,5},{6,7},{3,2},{5,4},{7,6},{8,9},{10,11},{12,13},{1... | collective-permute-start | bytes 1572872 | tf_op jit(solution)/shard_map/ppermute | solution.py:235
  23.7 5.3 %collective-permute-done.4.refs_4_ = bf16[2,128,512]{2,1,0:T(8,128)(2,1)S(1)} collective-permute-done((bf16[2,128,512]{2,1,0:T(8,128)(2,1)S(1)}, bf16[2,128,512]{2,1,0:T(8,128)(2,1)S(1)}, u32[]{:S(2)}, u32[]{:S(2)}) %collective-permute-start.4) | collective-permute-done | bytes 262176 | tf_op jit(solution)/shard_map/ppermute | solution.py:235
  29.0 1.6 %copy-done.4 = bf16[128,8192]{1,0:T(8,128)(2,1)S(1)} copy-done((bf16[128,8192]{1,0:T(8,128)(2,1)S(1)}, bf16[128,8192]{1,0:T(8,128)(2,1)}, u32[]{:S(2)}) %copy-start.4) | copy-done | bytes 2097176
  30.6 9.0 %attend.2 = (bf16[128,4096]{1,0:T(8,128)(2,1)S(1)}, f32[2,128,512]{2,1,0:T(8,128)S(1)}, bf16[2,128,512]{2,1,0:T(8,128)(2,1)S(1)}, bf16[2,128,512]{2,1,0:T(8,128)(2,1)S(1)}, bf16[2,2,128,512]{3,2,1,0:T(8,128)(2,1)}) custom-call(s32[8]{0:T(128)S(1)} %copy-done.22, bf16[128,8192]{1,0:T(8,128)(2,1)S(1)} %copy-done.2, bf16[128,8192]{1,0:T(8,128)(2,1)S(1)} %copy-done.4, ...), custom_call_target="tpu_custom_call" | custom-call | flops 13421772800 | bytes 7077888 | tf_op jit(solution)/shard_map/attend/pallas_call | solution.py:161
  41.4 1.3 %collective-permute-start.8 = (bf16[2,2,128,512]{3,2,1,0:T(8,128)(2,1)}, bf16[2,2,128,512]{3,2,1,0:T(8,128)(2,1)}, u32[]{:S(2)}, u32[]{:S(2)}) collective-permute-start(bf16[2,2,128,512]{3,2,1,0:T(8,128)(2,1)} %get-tuple-element.37), channel_id=1, source_target_pairs={{2,3},{4,5},{6,7},{1,0},{3,2},{5,4},{7,6},{10,11},{12,13},{14,15},... | collective-permute-start | bytes 1572872 | tf_op jit(solution)/shard_map/ppermute | solution.py:235
  44.6 8.4 %attend.3 = (bf16[128,4096]{1,0:T(8,128)(2,1)S(1)}, f32[2,128,512]{2,1,0:T(8,128)S(1)}, bf16[2,128,512]{2,1,0:T(8,128)(2,1)S(1)}, bf16[2,128,512]{2,1,0:T(8,128)...) custom-call(s32[8]{0:T(128)S(1)} %copy-done.22, bf16[128,8192]{1,0:T(8,128)(2,1)S(1)} %copy-done.2, ...), custom_call_target="tpu_custom_call" | custom-call | flops 13421772800 | bytes 7077888 | tf_op jit(solution)/shard_map/attend/pallas_call | solution.py:161
  55.9 1.4 %collective-permute-start.7 = (bf16[2,128,512]{2,1,0:T(8,128)(2,1)}, bf16[2,128,512]{2,1,0:T(8,128)(2,1)S(1)}, u32[]{:S(2)}, u32[]{:S(2)}) collective-permute-start(bf16[2,128,512]{2,1,0:T(8,128)(2,1)} %get-tuple-element.34), channel_id=1, source_target_pairs={{4,5},{6,7},{1,0},{3,2},{5,4},{7,6},{12,13},{14,15},{9,8},{11,10},... | collective-permute-start | bytes 786440 | tf_op jit(solution)/shard_map/ppermute | solution.py:235
  57.4 1.1 %fusion.6 = bf16[2,128,512]{2,1,0:T(8,128)(2,1)S(1)} fusion(bf16[2,128,512]{2,1,0:T(8,128)(2,1)} %copy-done.18, pred[]{:T(512)S(6)} %eq.10, bf16[2,2,128,512]{3,2,1,0:T(8,128)(2,1)} %collective-permute-done.8), kind=kLoop, calls=%fused_computation.9 | loop fusion | flops 655360 | bytes 786433 | tf_op jit(solution)/shard_map/convert_element_type | solution.py:290
  59.9 5.5 %collective-permute-done.7.refs_2_ = bf16[2,128,512]{2,1,0:T(8,128)(2,1)S(1)} collective-permute-done((bf16[2,128,512]{2,1,0:T(8,128)(2,1)}, bf16[2,128,512]{2,1,0:T(8,128)(2,1)S(1)}, u32[]{:S(2)}, u32[]{:S(2)}) %collective-permute-start.7) | collective-permute-done | bytes 262176 | tf_op jit(solution)/shard_map/ppermute | solution.py:235
  67.0 1.1 %fusion.8 = bf16[2,128,512]{2,1,0:T(8,128)(2,1)S(1)} fusion(bf16[2,128,512]{2,1,0:T(8,128)(2,1)S(1)} %collective-permute-done.9, bf16[2,128,512]{2,1,0:T(8,128)(2,1)} %copy-done.15, bf16[2,2,128,512]{3,2,1,0:T(8,128)(2,1)} %collective-permute-done.8), kind=kLoop, calls=%fused_computation.13 | loop fusion | flops 786432 | bytes 1048576 | tf_op jit(solution)/shard_map/convert_element_type | solution.py:290
  68.2 1.3 %collective-permute-start.10 = (bf16[2,128,512]{2,1,0:T(8,128)(2,1)S(1)}, bf16[2,128,512]{2,1,0:T(8,128)(2,1)S(1)}, u32[]{:S(2)}, u32[]{:S(2)}) collective-permute-start(bf16[2,128,512]{2,1,0:T(8,128)(2,1)S(1)} %fusion.8), channel_id=1, source_target_pairs={{2,0},{3,1},{4,2},{5,3},{6,4},{7,5},{10,8},{11,9},{12,10},{13,11},... | collective-permute-start | bytes 786440 | tf_op jit(solution)/shard_map/ppermute | solution.py:235
  69.6 1.3 %collective-permute-start.13 = (bf16[2,128,512]{2,1,0:T(8,128)(2,1)S(1)}, bf16[2,128,512]{2,1,0:T(8,128)(2,1)S(1)}, u32[]{:S(2)}, u32[]{:S(2)}) collective-permute-start(bf16[2,128,512]{2,1,0:T(8,128)(2,1)S(1)} %add_convert_fusion), channel_id=1, source_target_pairs={{2,0},{3,1},{4,2},{5,3},{6,4},{7,5},{10,8},{11,9},{12,10},{13,11},... | collective-permute-start | bytes 786440 | tf_op jit(solution)/shard_map/ppermute | solution.py:235
  70.9 1.5 %pad_maximum_fusion = bf16[128,8192]{1,0:T(8,128)(2,1)} fusion(bf16[128,4096]{1,0:T(8,128)(2,1)S(1)} %get-tuple-element.35, bf16[128,4096]{1,0:T(8,128)(2,1)S(1)} %copy-done.6), kind=kLoop, calls=%fused_computation | loop fusion | flops 4194304 | bytes 4194304 | tf_op jit(solution)/shard_map/concatenate | solution.py:304
  72.4 17.1 %collective-permute-done.10 = bf16[2,128,512]{2,1,0:T(8,128)(2,1)S(1)} collective-permute-done((bf16[2,128,512]{2,1,0:T(8,128)(2,1)S(1)}, bf16[2,128,512]{2,1,0:T(8,128)(2,1)S(1)}, u32[]{:S(2)}, u32[]{:S(2)}) %collective-permute-start.10) | collective-permute-done | bytes 262176 | tf_op jit(solution)/shard_map/ppermute | solution.py:235
  89.5 1.1 %fusion.3.refs_0_ = bf16[2,128,512]{2,1,0:T(8,128)(2,1)S(1)} fusion(f32[2,128,512]{2,1,0:T(8,128)S(1)} %copy-done.8, bf16[2,128,512]{2,1,0:T(8,128)(2,1)S(1)} %collective-permute-done.10, pred[]{:T(512)S(6)} %eq.4, bf16[2,2,128,512]{3,2,1,0:T(8,128)(2,1)} %collective-permute-done.8), kind=kLoop, calls=%fused_computation.6 | loop fusion | flops 786432 | bytes 1310721 | tf_op jit(solution)/shard_map/convert_element_type | solution.py:300
  90.6 4.0 %collective-permute-done.13.refs_3_ = bf16[2,128,512]{2,1,0:T(8,128)(2,1)S(1)} collective-permute-done((bf16[2,128,512]{2,1,0:T(8,128)(2,1)S(1)}, bf16[2,128,512]{2,1,0:T(8,128)(2,1)S(1)}, u32[]{:S(2)}, u32[]{:S(2)}) %collective-permute-start.13) | collective-permute-done | bytes 262176 | tf_op jit(solution)/shard_map/ppermute | solution.py:235
  (66 shorter events, 13.1 us)
Async XLA Ops:
  0.6 9.8 %copy-start = (bf16[128,8192]{1,0:T(8,128)(2,1)S(1)}, bf16[128,8192]{1,0:T(8,128)(2,1)}, u32[]{:S(2)}) copy-start(bf16[128,8192]{1,0:T(8,128)(2,1)} %out_ref.1) | copy-start | bytes 6291460
  2.0 13.2 %collective-permute-start.1 = (bf16[2,128,512]{2,1,0:T(8,128)(2,1)S(1)}, bf16[2,128,512]{2,1,0:T(8,128)(2,1)}, u32[]{:S(2)}, u32[]{:S(2)}) collective-permute-start(bf16[2,128,512]{2,1,0:T(8,128)(2,1)S(1)} %pad_maximum_fusion.3.refs_0_), channel_id=1, source_target_pairs={{0,2},{1,3},{2,4},{3,5},{4,6},{5,7},{8,10},{9,11},{10,12},{11,13},... | collective-permute-start | bytes 786440 | tf_op jit(solution)/shard_map/ppermute | solution.py:235
  7.6 10.4 %collective-permute-start = (bf16[2,128,512]{2,1,0:T(8,128)(2,1)S(1)}, bf16[2,128,512]{2,1,0:T(8,128)(2,1)S(1)}, u32[]{:S(2)}, u32[]{:S(2)}) collective-permute-start(bf16[2,128,512]{2,1,0:T(8,128)(2,1)S(1)} %pad_maximum_fusion.2.refs_0_), channel_id=1, source_target_pairs={{0,2},{1,3},{2,4},{3,5},{4,6},{5,7},{8,10},{9,11},{10,12},{11,13},... | collective-permute-start | bytes 786440 | tf_op jit(solution)/shard_map/ppermute | solution.py:235
  15.1 13.9 %copy-start.2 = (bf16[128,8192]{1,0:T(8,128)(2,1)S(1)}, bf16[128,8192]{1,0:T(8,128)(2,1)}, u32[]{:S(2)}) copy-start(bf16[128,8192]{1,0:T(8,128)(2,1)} %q_ref.5) | copy-start | bytes 6291460
  15.1 13.9 %copy-start.21 = (f32[128,64]{0,1:T(8,128)S(1)}, f32[128,64]{0,1:T(8,128)}, u32[]{:S(2)}) copy-start(f32[128,64]{0,1:T(8,128)} %param.12) | copy-start | bytes 98308
  15.1 13.9 %copy-start.22 = (s32[8]{0:T(128)S(1)}, s32[8]{0:T(128)}, u32[]{:S(2)}) copy-start(s32[8]{0:T(128)} %docs.3) | copy-start | bytes 100
  15.1 3.6 %collective-permute-start.2 = (bf16[2,128,512]{2,1,0:T(8,128)(2,1)}, bf16[2,128,512]{2,1,0:T(8,128)(2,1)S(1)}, u32[]{:S(2)}, u32[]{:S(2)}) collective-permute-start(bf16[2,128,512]{2,1,0:T(8,128)(2,1)} %collective-permute-done.1.refs_1_), channel_id=1, source_target_pairs={{2,4},{3,5},{4,6},{5,7},{10,12},{11,13},{12,14},{13,15},{18,20},{1... | collective-permute-start | bytes 786440 | tf_op jit(solution)/shard_map/ppermute | solution.py:235
  15.9 2.8 %collective-permute-start.3 = (bf16[2,128,512]{2,1,0:T(8,128)(2,1)}, bf16[2,128,512]{2,1,0:T(8,128)(2,1)}, u32[]{:S(2)}, u32[]{:S(2)}) collective-permute-start(bf16[2,128,512]{2,1,0:T(8,128)(2,1)} %collective-permute-done.1.refs_1_), channel_id=1, source_target_pairs={{2,3},{4,5},{6,7},{3,2},{5,4},{7,6},{10,11},{12,13},{14,15},{11,10... | collective-permute-start | bytes 786440 | tf_op jit(solution)/shard_map/ppermute | solution.py:235
  18.1 21.5 %copy-start.11 = (bf16[2,128,512]{2,1,0:T(8,128)(2,1)}, bf16[2,128,512]{2,1,0:T(8,128)(2,1)S(1)}, u32[]{:S(2)}) copy-start(bf16[2,128,512]{2,1,0:T(8,128)(2,1)S(1)} %collective-permute-done.refs_1_) | copy-start | bytes 786436
  18.1 4.2 %collective-permute-start.5 = (bf16[2,128,512]{2,1,0:T(8,128)(2,1)S(1)}, bf16[2,128,512]{2,1,0:T(8,128)(2,1)S(1)}, u32[]{:S(2)}, u32[]{:S(2)}) collective-permute-start(bf16[2,128,512]{2,1,0:T(8,128)(2,1)S(1)} %collective-permute-done.refs_1_), channel_id=1, source_target_pairs={{2,4},{3,5},{4,6},{5,7},{10,12},{11,13},{12,14},{13,15},{18,20},{1... | collective-permute-start | bytes 786440 | tf_op jit(solution)/shard_map/ppermute | solution.py:235
  18.8 10.2 %collective-permute-start.4 = (bf16[2,128,512]{2,1,0:T(8,128)(2,1)S(1)}, bf16[2,128,512]{2,1,0:T(8,128)(2,1)S(1)}, u32[]{:S(2)}, u32[]{:S(2)}) collective-permute-start(bf16[2,128,512]{2,1,0:T(8,128)(2,1)S(1)} %broadcast_select_fusion), channel_id=1, source_target_pairs={{0,1},{2,3},{4,5},{6,7},{5,4},{7,6},{8,9},{10,11},{12,13},{14,15},... | collective-permute-start | bytes 786440 | tf_op jit(solution)/shard_map/ppermute | solution.py:235
  22.3 17.3 %copy-start.13 = (bf16[2,128,512]{2,1,0:T(8,128)(2,1)}, bf16[2,128,512]{2,1,0:T(8,128)(2,1)S(1)}, u32[]{:S(2)}) copy-start(bf16[2,128,512]{2,1,0:T(8,128)(2,1)S(1)} %collective-permute-done.5.refs_2_) | copy-start | bytes 786436
  22.4 20.3 %collective-permute-start.6 = (bf16[2,2,128,512]{3,2,1,0:T(8,128)(2,1)S(1)}, bf16[2,2,128,512]{3,2,1,0:T(8,128)(2,1)S(1)}, u32[]{:S(2)}, u32[]{:S(2)}) collective-permute-start(bf16[2,2,128,512]{3,2,1,0:T(8,128)(2,1)S(1)} %pad_maximum_fusion.1), channel_id=1, source_target_pairs={{0,1},{2,3},{4,5},{6,7},{3,2},{5,4},{7,6},{8,9},{10,11},{12,13},{1... | collective-permute-start | bytes 1572872 | tf_op jit(solution)/shard_map/ppermute | solution.py:235
  41.4 16.0 %collective-permute-start.8 = (bf16[2,2,128,512]{3,2,1,0:T(8,128)(2,1)}, bf16[2,2,128,512]{3,2,1,0:T(8,128)(2,1)}, u32[]{:S(2)}, u32[]{:S(2)}) collective-permute-start(bf16[2,2,128,512]{3,2,1,0:T(8,128)(2,1)} %get-tuple-element.37), channel_id=1, source_target_pairs={{2,3},{4,5},{6,7},{1,0},{3,2},{5,4},{7,6},{10,11},{12,13},{14,15},... | collective-permute-start | bytes 1572872 | tf_op jit(solution)/shard_map/ppermute | solution.py:235
  55.9 15.0 %copy-start.6 = (bf16[128,4096]{1,0:T(8,128)(2,1)S(1)}, bf16[128,4096]{1,0:T(8,128)(2,1)}, u32[]{:S(2)}) copy-start(bf16[128,4096]{1,0:T(8,128)(2,1)} %copy-done.5) | copy-start | bytes 3145732
  55.9 13.6 %copy-start.17 = (bf16[2,128,512]{2,1,0:T(8,128)(2,1)S(1)}, bf16[2,128,512]{2,1,0:T(8,128)(2,1)}, u32[]{:S(2)}) copy-start(bf16[2,128,512]{2,1,0:T(8,128)(2,1)} %copy-done.16) | copy-start | bytes 786436
  55.9 9.4 %collective-permute-start.7 = (bf16[2,128,512]{2,1,0:T(8,128)(2,1)}, bf16[2,128,512]{2,1,0:T(8,128)(2,1)S(1)}, u32[]{:S(2)}, u32[]{:S(2)}) collective-permute-start(bf16[2,128,512]{2,1,0:T(8,128)(2,1)} %get-tuple-element.34), channel_id=1, source_target_pairs={{4,5},{6,7},{1,0},{3,2},{5,4},{7,6},{12,13},{14,15},{9,8},{11,10},... | collective-permute-start | bytes 786440 | tf_op jit(solution)/shard_map/ppermute | solution.py:235
  58.5 8.5 %collective-permute-start.9 = (bf16[2,128,512]{2,1,0:T(8,128)(2,1)S(1)}, bf16[2,128,512]{2,1,0:T(8,128)(2,1)S(1)}, u32[]{:S(2)}, u32[]{:S(2)}) collective-permute-start(bf16[2,128,512]{2,1,0:T(8,128)(2,1)S(1)} %fusion.6), channel_id=1, source_target_pairs={{4,2},{5,3},{6,4},{7,5},{12,10},{13,11},{14,12},{15,13},{20,18},{2... | collective-permute-start | bytes 786440 | tf_op jit(solution)/shard_map/ppermute | solution.py:235
  59.2 10.3 %collective-permute-start.11 = (bf16[2,128,512]{2,1,0:T(8,128)(2,1)}, bf16[2,128,512]{2,1,0:T(8,128)(2,1)S(1)}, u32[]{:S(2)}, u32[]{:S(2)}) collective-permute-start(bf16[2,128,512]{2,1,0:T(8,128)(2,1)} %copy-done.20), channel_id=1, source_target_pairs={{2,3},{4,5},{6,7},{3,2},{5,4},{7,6},{10,11},{12,13},{14,15},{11,10... | collective-permute-start | bytes 786440 | tf_op jit(solution)/shard_map/ppermute | solution.py:235
  66.3 3.1 %collective-permute-start.12 = (bf16[2,128,512]{2,1,0:T(8,128)(2,1)S(1)}, bf16[2,128,512]{2,1,0:T(8,128)(2,1)S(1)}, u32[]{:S(2)}, u32[]{:S(2)}) collective-permute-start(bf16[2,128,512]{2,1,0:T(8,128)(2,1)S(1)} %add_convert_fusion.1), channel_id=1, source_target_pairs={{4,2},{5,3},{6,4},{7,5},{12,10},{13,11},{14,12},{15,13},{20,18},{2... | collective-permute-start | bytes 786440 | tf_op jit(solution)/shard_map/ppermute | solution.py:235
  68.2 21.4 %collective-permute-start.10 = (bf16[2,128,512]{2,1,0:T(8,128)(2,1)S(1)}, bf16[2,128,512]{2,1,0:T(8,128)(2,1)S(1)}, u32[]{:S(2)}, u32[]{:S(2)}) collective-permute-start(bf16[2,128,512]{2,1,0:T(8,128)(2,1)S(1)} %fusion.8), channel_id=1, source_target_pairs={{2,0},{3,1},{4,2},{5,3},{6,4},{7,5},{10,8},{11,9},{12,10},{13,11},... | collective-permute-start | bytes 786440 | tf_op jit(solution)/shard_map/ppermute | solution.py:235
  69.6 25.0 %collective-permute-start.13 = (bf16[2,128,512]{2,1,0:T(8,128)(2,1)S(1)}, bf16[2,128,512]{2,1,0:T(8,128)(2,1)S(1)}, u32[]{:S(2)}, u32[]{:S(2)}) collective-permute-start(bf16[2,128,512]{2,1,0:T(8,128)(2,1)S(1)} %add_convert_fusion), channel_id=1, source_target_pairs={{2,0},{3,1},{4,2},{5,3},{6,4},{7,5},{10,8},{11,9},{12,10},{13,11},... | collective-permute-start | bytes 786440 | tf_op jit(solution)/shard_map/ppermute | solution.py:235
  70.9 18.6 %copy-start.8 = (f32[2,128,512]{2,1,0:T(8,128)S(1)}, f32[2,128,512]{2,1,0:T(8,128)}, u32[]{:S(2)}) copy-start(f32[2,128,512]{2,1,0:T(8,128)} %copy-done.7) | copy-start | bytes 1572868
  70.9 23.6 %copy-start.10 = (f32[2,128,512]{2,1,0:T(8,128)S(1)}, f32[2,128,512]{2,1,0:T(8,128)}, u32[]{:S(2)}) copy-start(f32[2,128,512]{2,1,0:T(8,128)} %copy-done.9) | copy-start | bytes 1572868
  (13 other events, 14.0 us)

commit v3 on v2

--- a/solution.py
+++ b/solution.py
@@ -85,6 +85,7 @@
         parts = refs[:slots]
     k_all, v_all, bias, prob, score = refs[-5:]
     rows = q_ref.shape[0]
+    heads = moved[0].shape[-1] // HDIM
     scale = 1.0 / HDIM**0.5
     me = lax.axis_index("seq")
 
@@ -100,7 +101,7 @@
         visible = (key <= token) & (key >= begin)
         bias[slot * rows : (slot + 1) * rows, :] = jnp.where(visible, 0.0, -1e30)
 
-    @pl.loop(0, moved[0].shape[-1] // HDIM)
+    @pl.loop(0, heads)
     def _(index):
         column = pl.ds(pl.multiple_of(index * HDIM, HDIM), HDIM)
         wide = pl.ds(pl.multiple_of((first + index) * GROUP * HDIM, GROUP * HDIM), GROUP * HDIM)
@@ -149,9 +150,9 @@
     slots = 2 * hops + 1
     local = pl.BlockSpec(memory_space=pltpu.VMEM)
     operands = [docs, queries, grad_out, lse, delta] + [array for array, index in moved]
+    in_specs = [pl.BlockSpec(memory_space=pltpu.SMEM)] + [local] * (len(operands) - 1)
     out_shape = [jax.ShapeDtypeStruct((rows, per * GROUP * HDIM), jnp.bfloat16)]
-    kinds = [jnp.float32] + [jnp.bfloat16] * hops
-    out_shape += [jax.ShapeDtypeStruct((2, rows, per * HDIM), kind) for kind in kinds]
+    out_shape += [jax.ShapeDtypeStruct((2, rows, per * HDIM), jnp.bfloat16)] * (hops + 1)
     if joined:
         out_shape += [jax.ShapeDtypeStruct((hops, 2, rows, per * HDIM), jnp.bfloat16)]
     else:
@@ -160,7 +161,7 @@
     places = [index for array, index in moved]
     return pl.pallas_call(
         functools.partial(attend_kernel, hops, joined, head, places),
-        in_specs=[pl.BlockSpec(memory_space=pltpu.SMEM)] + [local] * (len(operands) - 1),
+        in_specs=in_specs,
         out_specs=[local] * len(out_shape),
         scratch_shapes=[
             pltpu.VMEM((slots * rows, HDIM), jnp.bfloat16),
@@ -218,6 +219,7 @@
     seq = lax.axis_size("seq")
     me = lax.axis_index("seq").astype(jnp.int32)
     side = lax.rem(me, 2)
+    keys, values, even, odd = lax.optimization_barrier((keys, values, side == 0, side == 1))
     hops = seq // 4
     def onward(hop):
         return [(s, s + 2) for s in range(2 * hop - 2, seq - 2)]
@@ -243,7 +245,8 @@
     columns = []
     for head, per in zip(heads, CHUNKS):
         at = slice(head * HDIM, (head + per) * HDIM)
-        own = lax.optimization_barrier(jnp.stack([keys[:, at], values[:, at]]))
+        own = jnp.stack([keys[:, at], values[:, at]])
+        own = lax.optimization_barrier(own)
         columns.append([own, send(own, onward(1))])
         columns[-1][1], delta = lax.optimization_barrier((columns[-1][1], delta))
     for column in columns:
@@ -251,7 +254,7 @@
             column.append(send(column[-1], onward(hop)))
     arrived = []
     for chunk, column in enumerate(columns):
-        edge = jnp.where(side == 0, column[0], column[hops])
+        edge = jnp.where(even, column[0], column[hops])
         moved = [(array, None) for array in column]
         if chunk == 0:
             crossed = [send(array, to_odd(1) + to_even(1)) for array in column[1:hops]]
@@ -273,7 +276,7 @@
         )
         grads_q.append(grad_q)
         outputs_of.append((parts[: hops + 1], parts[hops + 1 :], joined))
-    before = []
+    swapped = []
     for column, crossed, joined in outputs_of:
         if joined:
             crossed = send(crossed[0], to_odd(1) + to_even(0))
@@ -282,21 +285,27 @@
         else:
             edge = send(crossed[-1], to_odd(hops) + to_even(0))
             crossed = [
-                send(after(crossed[hop - 1], before[0]), to_odd(hop) + to_even(hop)) for hop in range(1, hops)
+                send(after(crossed[hop - 1], swapped[0][2]), to_odd(hop) + to_even(hop))
+                for hop in range(1, hops)
             ]
         edge = edge.astype(wide)
-        total = column[hops].astype(wide) + jnp.where(side == 1, edge, 0.0)
+        total = column[hops].astype(wide) + jnp.where(odd, edge, 0.0)
+        swapped.append((crossed, edge, total.astype(half)))
+    before = []
+    for (column, _, joined), (crossed, edge, total) in zip(outputs_of, swapped):
         for hop in range(hops - 1, -1, -1):
-            total = total.astype(half)
             if joined:
+                if hop == 0 and hops > 1:
+                    total = after(total, *swapped[-1][0])
                 before.append(total)
             elif hop == 0:
                 total = after(total, *before)
             far = send(total, back(hop + 1)).astype(wide)
             if hop:
                 total = column[hop].astype(wide) + crossed[hop - 1].astype(wide) + far
+                total = total.astype(half)
         if joined:
-            total = column[0] + jnp.where(side == 0, edge, 0.0) + far
+            total = column[0].astype(wide) + jnp.where(even, edge, 0.0) + far
             sums.append([total.astype(half)])
         else:
             sums.append([column[0], edge.astype(half), far.astype(half)])

time: 96.2 us -> 85.3 us (0.89)
  local copies, waits for them, and re-layouts: 12.7 us -> 4.47 us
  other arithmetic: 6.08 us -> 2.13 us
  waiting for transfers between devices: 32.6 us -> 36.3 us
  Pallas kernels: 19.7 us -> 18.3 us
    unnamed x46 -> x12, local copies, waits for them, and re-layouts: 11.4 us -> 3.19 us
    ppermute x14, waiting for transfers between devices: 32.6 us -> 36.3 us  [send(): return lax.ppermute(array, 'seq', pairs)]
    convert_element_type x4 -> x2, other arithmetic: 3.38 us -> 0.21 us  [shards(): total = total.astype(half)]
    pallas_call x2, Pallas kernels: 17.4 us -> 16 us  [attend(): pl.pallas_call(functools.partial(attend_kernel, hops, joined, head, place...]
  transfers between devices with their start and end apart: 14 -> 14, of which waited for: 5 -> 6; matrix products, arithmetic and copies ran while one was open for 6% -> 2% of each run, Pallas kernels for 20% -> 21%
where the time goes in v3:
time: 85.3 us; the launch traced here: 84.7 us
  waiting for transfers between devices  36.3 us (43%)
  starting transfers between devices  22.6 us (26%)
  Pallas kernels  18.3 us (21%)
  local copies, waits for them, and re-layouts  4.47 us (5%)
  other arithmetic  2.13 us (2%)
  between operations  0.93 us (1%)
    ppermute x14, waiting for transfers between devices, send(): return lax.ppermute(array, 'seq', pairs)  36.3 us
    ppermute x14, starting transfers between devices, send(): return lax.ppermute(array, 'seq', pairs)  22.6 us
    pallas_call x2, Pallas kernels, attend(): pl.pallas_call(functools.partial(attend_kernel, hops, joined, head, place...  16 us
    unnamed x12, local copies, waits for them, and re-layouts  3.19 us
  transfers between devices with their start and end apart: 14, of which 6 were waited for; matrix products, arithmetic and copies ran while one was open for 2% of the time, Pallas kernels for 21%

profile of v3, /device:TPU:0, one launch (start us, length us, event | category | flops | bytes accessed | tf_op | source)
XLA Modules:
  0.0 84.7 jit_solution(3042824876885129206)
XLA Ops:
  0.6 1.3 %slice_bitcast_fusion = (bf16[1,128,512]{2,1,0:T(8,128)(2,1)S(1)}, bf16[1,128,512]{2,1,0:T(8,128)(2,1)S(1)}, bf16[1,128,512]{2,1,0:T(8,128)(2,1)S(1)}, bf16[1,128,512]{2,1,0:T(8,128)(2,1)S(1)}) fusion(bf16[128,1024]{1,0:T(8,128)(2,1)} %param.9, bf16[128,1024]{1,0:T(8,128)(2,1)} %param.8), kind=kLoop, calls=%fused_computation.20 | loop fusion | bytes 1048576 | tf_op jit(solution)/shard_map/stack | solution.py:248
  2.0 4.9 %collective-permute-start.1 = (bf16[2,128,512]{2,1,0:T(8,128)(2,1)S(1)}, bf16[2,128,512]{2,1,0:T(8,128)(2,1)S(1)}, u32[]{:S(2)}, u32[]{:S(2)}) collective-permute-start(bf16[2,128,512]{2,1,0:T(8,128)(2,1)S(1)} %pad_maximum_fusion.3.refs_0_), channel_id=1, source_target_pairs={{0,2},{1,3},{2,4},{3,5},{4,6},{5,7},{8,10},{9,11},{10,12},{11,13},... | collective-permute-start | bytes 786440 | tf_op jit(solution)/shard_map/ppermute | solution.py:237
  7.0 3.5 %collective-permute-start = (bf16[2,128,512]{2,1,0:T(8,128)(2,1)S(1)}, bf16[2,128,512]{2,1,0:T(8,128)(2,1)S(1)}, u32[]{:S(2)}, u32[]{:S(2)}) collective-permute-start(bf16[2,128,512]{2,1,0:T(8,128)(2,1)S(1)} %pad_maximum_fusion.2.refs_0_), channel_id=1, source_target_pairs={{0,2},{1,3},{2,4},{3,5},{4,6},{5,7},{8,10},{9,11},{10,12},{11,13},... | collective-permute-start | bytes 786440 | tf_op jit(solution)/shard_map/ppermute | solution.py:237
  10.5 1.6 %copy-done.1 = bf16[128,8192]{1,0:T(8,128)(2,1)S(1)} copy-done((bf16[128,8192]{1,0:T(8,128)(2,1)S(1)}, bf16[128,8192]{1,0:T(8,128)(2,1)}, u32[]{:S(2)}) %copy-start.1) | copy-done | bytes 2097176
  12.0 1.6 %copy-done.3 = bf16[128,8192]{1,0:T(8,128)(2,1)S(1)} copy-done((bf16[128,8192]{1,0:T(8,128)(2,1)S(1)}, bf16[128,8192]{1,0:T(8,128)(2,1)}, u32[]{:S(2)}) %copy-start.3) | copy-done | bytes 2097176
  13.6 1.5 %delta.1.delta_ref = f32[64,128]{1,0:T(8,128)S(1)} custom-call(bf16[128,8192]{1,0:T(8,128)(2,1)S(1)} %copy-done, bf16[128,8192]{1,0:T(8,128)(2,1)S(1)} %copy-done.3, bf16[128,8192]{1,0:T(8,128)(2,1)S(1)} %copy-done.1), custom_call_target="tpu_custom_call" | custom-call | flops 536870912 | bytes 6291456 | tf_op jit(solution)/shard_map/delta/pallas_call | solution.py:55
  15.1 0.8 collective-permute-start.2
  16.6 1.4 %collective-permute-done.refs_1_ = bf16[2,128,512]{2,1,0:T(8,128)(2,1)S(1)} collective-permute-done((bf16[2,128,512]{2,1,0:T(8,128)(2,1)S(1)}, bf16[2,128,512]{2,1,0:T(8,128)(2,1)S(1)}, u32[]{:S(2)}, u32[]{:S(2)}) %collective-permute-start) | collective-permute-done | bytes 262176 | tf_op jit(solution)/shard_map/ppermute | solution.py:237
  18.8 3.5 %collective-permute-start.4 = (bf16[2,128,512]{2,1,0:T(8,128)(2,1)S(1)}, bf16[2,128,512]{2,1,0:T(8,128)(2,1)S(1)}, u32[]{:S(2)}, u32[]{:S(2)}) collective-permute-start(bf16[2,128,512]{2,1,0:T(8,128)(2,1)S(1)} %broadcast_select_fusion), channel_id=1, source_target_pairs={{0,1},{2,3},{4,5},{6,7},{5,4},{7,6},{8,9},{10,11},{12,13},{14,15},... | collective-permute-start | bytes 786440 | tf_op jit(solution)/shard_map/ppermute | solution.py:237
  22.4 1.3 %collective-permute-start.6 = (bf16[2,2,128,512]{3,2,1,0:T(8,128)(2,1)S(1)}, bf16[2,2,128,512]{3,2,1,0:T(8,128)(2,1)S(1)}, u32[]{:S(2)}, u32[]{:S(2)}) collective-permute-start(bf16[2,2,128,512]{3,2,1,0:T(8,128)(2,1)S(1)} %pad_maximum_fusion.1), channel_id=1, source_target_pairs={{0,1},{2,3},{4,5},{6,7},{3,2},{5,4},{7,6},{8,9},{10,11},{12,13},{1... | collective-permute-start | bytes 1572872 | tf_op jit(solution)/shard_map/ppermute | solution.py:237
  23.7 5.3 %collective-permute-done.4.refs_4_ = bf16[2,128,512]{2,1,0:T(8,128)(2,1)S(1)} collective-permute-done((bf16[2,128,512]{2,1,0:T(8,128)(2,1)S(1)}, bf16[2,128,512]{2,1,0:T(8,128)(2,1)S(1)}, u32[]{:S(2)}, u32[]{:S(2)}) %collective-permute-start.4) | collective-permute-done | bytes 262176 | tf_op jit(solution)/shard_map/ppermute | solution.py:237
  29.0 8.0 %attend.2 = (bf16[128,4096]{1,0:T(8,128)(2,1)S(1)}, bf16[2,128,512]{2,1,0:T(8,128)(2,1)S(1)}, bf16[2,128,512]{2,1,0:T(8,128)(2,1)S(1)}, bf16[2,128,512]{2,1,0:T(8,128)(2,1)S(1)}, bf16[2,2,128,512]{3,2,1,0:T(8,128)(2,1)S(1)}) custom-call(s32[8]{0:T(128)S(1)} %copy-done.5, bf16[128,8192]{1,0:T(8,128)(2,1)S(1)} %copy-done.2, bf16[128,8192]{1,0:T(8,128)(2,1)S(1)} %copy-done.3, ...), custom_call_target="tpu_custom_call" | custom-call | flops 13421772800 | bytes 7077888 | tf_op jit(solution)/shard_map/attend/pallas_call | solution.py:162
  37.0 1.3 %collective-permute-start.8 = (bf16[2,2,128,512]{3,2,1,0:T(8,128)(2,1)S(1)}, bf16[2,2,128,512]{3,2,1,0:T(8,128)(2,1)S(1)}, u32[]{:S(2)}, u32[]{:S(2)}) collective-permute-start(bf16[2,2,128,512]{3,2,1,0:T(8,128)(2,1)S(1)} %get-tuple-element.45), channel_id=1, source_target_pairs={{2,3},{4,5},{6,7},{1,0},{3,2},{5,4},{7,6},{10,11},{12,13},{14,15},... | collective-permute-start | bytes 1572872 | tf_op jit(solution)/shard_map/ppermute | solution.py:237
  38.3 8.0 %attend.3 = (bf16[128,4096]{1,0:T(8,128)(2,1)S(1)}, bf16[2,128,512]{2,1,0:T(8,128)(2,1)S(1)}, bf16[2,128,512]{2,1,0:T(8,128)(2,1)S(1)}, bf16[2,128,512]{2,1,0:T(...) custom-call(s32[8]{0:T(128)S(1)} %copy-done.5, bf16[128,8192]{1,0:T(8,128)(2,1)S(1)} %copy-done.2, ...), custom_call_target="tpu_custom_call" | custom-call | flops 13421772800 | bytes 7077888 | tf_op jit(solution)/shard_map/attend/pallas_call | solution.py:162
  46.3 1.3 %collective-permute-start.7 = (bf16[2,128,512]{2,1,0:T(8,128)(2,1)S(1)}, bf16[2,128,512]{2,1,0:T(8,128)(2,1)S(1)}, u32[]{:S(2)}, u32[]{:S(2)}) collective-permute-start(bf16[2,128,512]{2,1,0:T(8,128)(2,1)S(1)} %get-tuple-element.42), channel_id=1, source_target_pairs={{4,5},{6,7},{1,0},{3,2},{5,4},{7,6},{12,13},{14,15},{9,8},{11,10},... | collective-permute-start | bytes 786440 | tf_op jit(solution)/shard_map/ppermute | solution.py:237
  47.6 1.2 %collective-permute-done.8 = bf16[2,2,128,512]{3,2,1,0:T(8,128)(2,1)S(1)} collective-permute-done((bf16[2,2,128,512]{3,2,1,0:T(8,128)(2,1)S(1)}, bf16[2,2,128,512]{3,2,1,0:T(8,128)(2,1)S(1)}, u32[]{:S(2)}, u32[]{:S(2)}) %collective-permute-start.8) | collective-permute-done | bytes 524320 | tf_op jit(solution)/shard_map/ppermute | solution.py:237
  48.9 0.7 collective-permute-start.9
  50.2 4.4 %collective-permute-done.7.refs_2_ = bf16[2,128,512]{2,1,0:T(8,128)(2,1)S(1)} collective-permute-done((bf16[2,128,512]{2,1,0:T(8,128)(2,1)S(1)}, bf16[2,128,512]{2,1,0:T(8,128)(2,1)S(1)}, u32[]{:S(2)}, u32[]{:S(2)}) %collective-permute-start.7) | collective-permute-done | bytes 262176 | tf_op jit(solution)/shard_map/ppermute | solution.py:237
  55.5 1.3 %collective-permute-start.11 = (bf16[2,128,512]{2,1,0:T(8,128)(2,1)S(1)}, bf16[2,128,512]{2,1,0:T(8,128)(2,1)S(1)}, u32[]{:S(2)}, u32[]{:S(2)}) collective-permute-start(bf16[2,128,512]{2,1,0:T(8,128)(2,1)S(1)} %fusion.8), channel_id=1, source_target_pairs={{2,0},{3,1},{4,2},{5,3},{6,4},{7,5},{10,8},{11,9},{12,10},{13,11},... | collective-permute-start | bytes 786440 | tf_op jit(solution)/shard_map/ppermute | solution.py:237
  56.9 1.3 %collective-permute-start.13 = (bf16[2,128,512]{2,1,0:T(8,128)(2,1)S(1)}, bf16[2,128,512]{2,1,0:T(8,128)(2,1)S(1)}, u32[]{:S(2)}, u32[]{:S(2)}) collective-permute-start(bf16[2,128,512]{2,1,0:T(8,128)(2,1)S(1)} %add_convert_fusion), channel_id=1, source_target_pairs={{2,0},{3,1},{4,2},{5,3},{6,4},{7,5},{10,8},{11,9},{12,10},{13,11},... | collective-permute-start | bytes 786440 | tf_op jit(solution)/shard_map/ppermute | solution.py:237
  58.2 1.5 %pad_maximum_fusion = bf16[128,8192]{1,0:T(8,128)(2,1)} fusion(bf16[128,4096]{1,0:T(8,128)(2,1)S(1)} %get-tuple-element.43, bf16[128,4096]{1,0:T(8,128)(2,1)S(1)} %get-tuple-element.40), kind=kLoop, calls=%fused_computation | loop fusion | flops 4194304 | bytes 4194304 | tf_op jit(solution)/shard_map/concatenate | solution.py:313
  59.7 19.4 %collective-permute-done.11 = bf16[2,128,512]{2,1,0:T(8,128)(2,1)S(1)} collective-permute-done((bf16[2,128,512]{2,1,0:T(8,128)(2,1)S(1)}, bf16[2,128,512]{2,1,0:T(8,128)(2,1)S(1)}, u32[]{:S(2)}, u32[]{:S(2)}) %collective-permute-start.11) | collective-permute-done | bytes 262176 | tf_op jit(solution)/shard_map/ppermute | solution.py:237
  79.2 4.7 %collective-permute-done.13.refs_3_ = bf16[2,128,512]{2,1,0:T(8,128)(2,1)S(1)} collective-permute-done((bf16[2,128,512]{2,1,0:T(8,128)(2,1)S(1)}, bf16[2,128,512]{2,1,0:T(8,128)(2,1)S(1)}, u32[]{:S(2)}, u32[]{:S(2)}) %collective-permute-start.13) | collective-permute-done | bytes 262176 | tf_op jit(solution)/shard_map/ppermute | solution.py:237
  83.9 0.9 %finish.1 = (bf16[128,1024]{1,0:T(8,128)(2,1)}, bf16[128,1024]{1,0:T(8,128)(2,1)}) custom-call(bf16[2,128,512]{2,1,0:T(8,128)(2,1)S(1)} %fusion.3.refs_0_, bf16[2,128,512]{2,1,0:T(8,128)(2,1)S(1)} %get-tuple-element.53.refs_1_, bf16[2,128,512]{2,1,0:T(8,128)(2,1)S(1)} %collective-permute-done.7.refs_2_, bf16[2,128,512]{2,1,0:T(8,128)(2,1)S(1)} %collective-permute-done.13.refs_3_), custom_call_target="tpu_custom_call" | custom-call | flops 1048576 | bytes 2097152 | tf_op jit(solution)/shard_map/finish/pallas_call | solution.py:205
  (32 shorter events, 3.4 us)
Async XLA Ops:
  0.6 9.8 %copy-start = (bf16[128,8192]{1,0:T(8,128)(2,1)S(1)}, bf16[128,8192]{1,0:T(8,128)(2,1)}, u32[]{:S(2)}) copy-start(bf16[128,8192]{1,0:T(8,128)(2,1)} %out_ref.1) | copy-start | bytes 6291460
  2.0 13.2 %collective-permute-start.1 = (bf16[2,128,512]{2,1,0:T(8,128)(2,1)S(1)}, bf16[2,128,512]{2,1,0:T(8,128)(2,1)S(1)}, u32[]{:S(2)}, u32[]{:S(2)}) collective-permute-start(bf16[2,128,512]{2,1,0:T(8,128)(2,1)S(1)} %pad_maximum_fusion.3.refs_0_), channel_id=1, source_target_pairs={{0,2},{1,3},{2,4},{3,5},{4,6},{5,7},{8,10},{9,11},{10,12},{11,13},... | collective-permute-start | bytes 786440 | tf_op jit(solution)/shard_map/ppermute | solution.py:237
  7.0 11.1 %collective-permute-start = (bf16[2,128,512]{2,1,0:T(8,128)(2,1)S(1)}, bf16[2,128,512]{2,1,0:T(8,128)(2,1)S(1)}, u32[]{:S(2)}, u32[]{:S(2)}) collective-permute-start(bf16[2,128,512]{2,1,0:T(8,128)(2,1)S(1)} %pad_maximum_fusion.2.refs_0_), channel_id=1, source_target_pairs={{0,2},{1,3},{2,4},{3,5},{4,6},{5,7},{8,10},{9,11},{10,12},{11,13},... | collective-permute-start | bytes 786440 | tf_op jit(solution)/shard_map/ppermute | solution.py:237
  10.5 1.6 %copy-start.1 = (bf16[128,8192]{1,0:T(8,128)(2,1)S(1)}, bf16[128,8192]{1,0:T(8,128)(2,1)}, u32[]{:S(2)}) copy-start(bf16[128,8192]{1,0:T(8,128)(2,1)} %q_ref.5) | copy-start | bytes 6291460
  12.0 1.6 %copy-start.3 = (bf16[128,8192]{1,0:T(8,128)(2,1)S(1)}, bf16[128,8192]{1,0:T(8,128)(2,1)}, u32[]{:S(2)}) copy-start(bf16[128,8192]{1,0:T(8,128)(2,1)} %gout_ref.5) | copy-start | bytes 6291460
  15.1 13.9 %copy-start.2 = (bf16[128,8192]{1,0:T(8,128)(2,1)S(1)}, bf16[128,8192]{1,0:T(8,128)(2,1)}, u32[]{:S(2)}) copy-start(bf16[128,8192]{1,0:T(8,128)(2,1)} %q_ref.5) | copy-start | bytes 6291460
  15.1 13.9 %copy-start.4 = (f32[128,64]{0,1:T(8,128)S(1)}, f32[128,64]{0,1:T(8,128)}, u32[]{:S(2)}) copy-start(f32[128,64]{0,1:T(8,128)} %param.12) | copy-start | bytes 98308
  15.1 13.9 %copy-start.5 = (s32[8]{0:T(128)S(1)}, s32[8]{0:T(128)}, u32[]{:S(2)}) copy-start(s32[8]{0:T(128)} %docs.3) | copy-start | bytes 100
  15.1 3.6 %collective-permute-start.2 = (bf16[2,128,512]{2,1,0:T(8,128)(2,1)S(1)}, bf16[2,128,512]{2,1,0:T(8,128)(2,1)S(1)}, u32[]{:S(2)}, u32[]{:S(2)}) collective-permute-start(bf16[2,128,512]{2,1,0:T(8,128)(2,1)S(1)} %collective-permute-done.1.refs_1_), channel_id=1, source_target_pairs={{2,4},{3,5},{4,6},{5,7},{10,12},{11,13},{12,14},{13,15},{18,20},{1... | collective-permute-start | bytes 786440 | tf_op jit(solution)/shard_map/ppermute | solution.py:237
  16.0 2.8 %collective-permute-start.3 = (bf16[2,128,512]{2,1,0:T(8,128)(2,1)S(1)}, bf16[2,128,512]{2,1,0:T(8,128)(2,1)S(1)}, u32[]{:S(2)}, u32[]{:S(2)}) collective-permute-start(bf16[2,128,512]{2,1,0:T(8,128)(2,1)S(1)} %collective-permute-done.1.refs_1_), channel_id=1, source_target_pairs={{2,3},{4,5},{6,7},{3,2},{5,4},{7,6},{10,11},{12,13},{14,15},{11,10... | collective-permute-start | bytes 786440 | tf_op jit(solution)/shard_map/ppermute | solution.py:237
  18.1 4.2 %collective-permute-start.5 = (bf16[2,128,512]{2,1,0:T(8,128)(2,1)S(1)}, bf16[2,128,512]{2,1,0:T(8,128)(2,1)S(1)}, u32[]{:S(2)}, u32[]{:S(2)}) collective-permute-start(bf16[2,128,512]{2,1,0:T(8,128)(2,1)S(1)} %collective-permute-done.refs_1_), channel_id=1, source_target_pairs={{2,4},{3,5},{4,6},{5,7},{10,12},{11,13},{12,14},{13,15},{18,20},{1... | collective-permute-start | bytes 786440 | tf_op jit(solution)/shard_map/ppermute | solution.py:237
  18.8 10.2 %collective-permute-start.4 = (bf16[2,128,512]{2,1,0:T(8,128)(2,1)S(1)}, bf16[2,128,512]{2,1,0:T(8,128)(2,1)S(1)}, u32[]{:S(2)}, u32[]{:S(2)}) collective-permute-start(bf16[2,128,512]{2,1,0:T(8,128)(2,1)S(1)} %broadcast_select_fusion), channel_id=1, source_target_pairs={{0,1},{2,3},{4,5},{6,7},{5,4},{7,6},{8,9},{10,11},{12,13},{14,15},... | collective-permute-start | bytes 786440 | tf_op jit(solution)/shard_map/ppermute | solution.py:237
  22.4 15.9 %collective-permute-start.6 = (bf16[2,2,128,512]{3,2,1,0:T(8,128)(2,1)S(1)}, bf16[2,2,128,512]{3,2,1,0:T(8,128)(2,1)S(1)}, u32[]{:S(2)}, u32[]{:S(2)}) collective-permute-start(bf16[2,2,128,512]{3,2,1,0:T(8,128)(2,1)S(1)} %pad_maximum_fusion.1), channel_id=1, source_target_pairs={{0,1},{2,3},{4,5},{6,7},{3,2},{5,4},{7,6},{8,9},{10,11},{12,13},{1... | collective-permute-start | bytes 1572872 | tf_op jit(solution)/shard_map/ppermute | solution.py:237
  37.0 11.8 %collective-permute-start.8 = (bf16[2,2,128,512]{3,2,1,0:T(8,128)(2,1)S(1)}, bf16[2,2,128,512]{3,2,1,0:T(8,128)(2,1)S(1)}, u32[]{:S(2)}, u32[]{:S(2)}) collective-permute-start(bf16[2,2,128,512]{3,2,1,0:T(8,128)(2,1)S(1)} %get-tuple-element.45), channel_id=1, source_target_pairs={{2,3},{4,5},{6,7},{1,0},{3,2},{5,4},{7,6},{10,11},{12,13},{14,15},... | collective-permute-start | bytes 1572872 | tf_op jit(solution)/shard_map/ppermute | solution.py:237
  46.3 8.3 %collective-permute-start.7 = (bf16[2,128,512]{2,1,0:T(8,128)(2,1)S(1)}, bf16[2,128,512]{2,1,0:T(8,128)(2,1)S(1)}, u32[]{:S(2)}, u32[]{:S(2)}) collective-permute-start(bf16[2,128,512]{2,1,0:T(8,128)(2,1)S(1)} %get-tuple-element.42), channel_id=1, source_target_pairs={{4,5},{6,7},{1,0},{3,2},{5,4},{7,6},{12,13},{14,15},{9,8},{11,10},... | collective-permute-start | bytes 786440 | tf_op jit(solution)/shard_map/ppermute | solution.py:237
  48.9 6.5 %collective-permute-start.9 = (bf16[2,128,512]{2,1,0:T(8,128)(2,1)S(1)}, bf16[2,128,512]{2,1,0:T(8,128)(2,1)S(1)}, u32[]{:S(2)}, u32[]{:S(2)}) collective-permute-start(bf16[2,128,512]{2,1,0:T(8,128)(2,1)S(1)} %fusion.6), channel_id=1, source_target_pairs={{4,2},{5,3},{6,4},{7,5},{12,10},{13,11},{14,12},{15,13},{20,18},{2... | collective-permute-start | bytes 786440 | tf_op jit(solution)/shard_map/ppermute | solution.py:237
  49.5 5.9 %collective-permute-start.10 = (bf16[2,128,512]{2,1,0:T(8,128)(2,1)S(1)}, bf16[2,128,512]{2,1,0:T(8,128)(2,1)S(1)}, u32[]{:S(2)}, u32[]{:S(2)}) collective-permute-start(bf16[2,128,512]{2,1,0:T(8,128)(2,1)S(1)} %get-tuple-element.51), channel_id=1, source_target_pairs={{2,3},{4,5},{6,7},{3,2},{5,4},{7,6},{10,11},{12,13},{14,15},{11,10... | collective-permute-start | bytes 786440 | tf_op jit(solution)/shard_map/ppermute | solution.py:237
  54.7 2.1 %collective-permute-start.12 = (bf16[2,128,512]{2,1,0:T(8,128)(2,1)S(1)}, bf16[2,128,512]{2,1,0:T(8,128)(2,1)S(1)}, u32[]{:S(2)}, u32[]{:S(2)}) collective-permute-start(bf16[2,128,512]{2,1,0:T(8,128)(2,1)S(1)} %add_convert_fusion.1), channel_id=1, source_target_pairs={{4,2},{5,3},{6,4},{7,5},{12,10},{13,11},{14,12},{15,13},{20,18},{2... | collective-permute-start | bytes 786440 | tf_op jit(solution)/shard_map/ppermute | solution.py:237
  55.5 23.6 %collective-permute-start.11 = (bf16[2,128,512]{2,1,0:T(8,128)(2,1)S(1)}, bf16[2,128,512]{2,1,0:T(8,128)(2,1)S(1)}, u32[]{:S(2)}, u32[]{:S(2)}) collective-permute-start(bf16[2,128,512]{2,1,0:T(8,128)(2,1)S(1)} %fusion.8), channel_id=1, source_target_pairs={{2,0},{3,1},{4,2},{5,3},{6,4},{7,5},{10,8},{11,9},{12,10},{13,11},... | collective-permute-start | bytes 786440 | tf_op jit(solution)/shard_map/ppermute | solution.py:237
  56.9 27.0 %collective-permute-start.13 = (bf16[2,128,512]{2,1,0:T(8,128)(2,1)S(1)}, bf16[2,128,512]{2,1,0:T(8,128)(2,1)S(1)}, u32[]{:S(2)}, u32[]{:S(2)}) collective-permute-start(bf16[2,128,512]{2,1,0:T(8,128)(2,1)S(1)} %add_convert_fusion), channel_id=1, source_target_pairs={{2,0},{3,1},{4,2},{5,3},{6,4},{7,5},{10,8},{11,9},{12,10},{13,11},... | collective-permute-start | bytes 786440 | tf_op jit(solution)/shard_map/ppermute | solution.py:237
